TPU v7x, 128 devices: a whole 4x4x4 slice. The times are simulated.
128 devices in a mesh: batch: 8 (over y_lo, x), blk: 16 (over y_hi, z, core).
Axes of the slice: x: 4, y: 4 (y_hi: 2, y_lo: 2; y = y_hi * 2 + y_lo), z: 4, core: 2. Of those that a mesh axis runs over, the one named last changes fastest.
Arguments:
- frames: bfloat16 [16, 2048, 1024], P('batch', 'blk'), may hold values from -6 to 6
- time_embed: bfloat16 [16, 1024], P('batch'), may hold values from -6 to 6
- segments: int32 [16, 2048], P('batch', 'blk'), may hold values from 0 to 5, as said below
- w_mod: bfloat16 [1024, 6144], replicated, may hold values from -0.1875 to 0.1875
- b_mod: bfloat16 [6144], replicated, may hold values from -4 to 4
- w_qkv: bfloat16 [1024, 3072], replicated, may hold values from -0.1875 to 0.1875
- b_qkv: bfloat16 [3072], replicated, may hold values from -4 to 4
- w_out: bfloat16 [1024, 1024], replicated, may hold values from -2 to 2
- b_out: bfloat16 [1024], replicated, may hold values from -6 to 6
- w_up: bfloat16 [1024, 2048], replicated, may hold values from -0.1875 to 0.1875
- b_up: bfloat16 [2048], replicated, may hold values from -4 to 4
- w_down: bfloat16 [2048, 1024], replicated, may hold values from -0.125 to 0.125
- b_down: bfloat16 [1024], replicated, may hold values from -6 to 6
- cotangent: bfloat16 [16, 2048, 1024], P('batch', 'blk'), may hold values from -6 to 6
Outputs:
- out_frames: bfloat16 [16, 2048, 1024], P('batch', 'blk')
- grad_frames: float32 [16, 2048, 1024], P('batch', 'blk')
- grad_time: float32 [16, 1024], P('batch')
- grad_w_mod: float32 [1024, 6144], P(('batch', 'blk'))
- grad_b_mod: float32 [6144], P(('batch', 'blk'))
- grad_w_qkv: float32 [1024, 3072], P(('batch', 'blk'))
- grad_b_qkv: float32 [3072], P(('batch', 'blk'))
- grad_w_out: float32 [1024, 1024], P(('batch', 'blk'))
- grad_b_out: float32 [1024], P(('batch', 'blk'))
- grad_w_up: float32 [1024, 2048], P(('batch', 'blk'))
- grad_b_up: float32 [2048], P(('batch', 'blk'))
- grad_w_down: float32 [2048, 1024], P(('batch', 'blk'))
- grad_b_down: float32 [1024], P(('batch', 'blk'))
Inputs may be any that keep to these rules, and one draw needn't show every extreme that they name: Segment numbers start at 0 and never fall along a row. In each aligned group of 2 rows, one row holds segments 0, 1 and 2, with segment 1 beginning within the first 128 frames and ending within the last 128 frames of its row; every other row packs 2 to 6 utterances.
All inputs are finite; a program needn't handle non-finite values.
Results may differ from a plain program's by a relative error of at most 0.018.
Values may be sent and summed in bfloat16 or wider, within the bound.
No kernel may reach another device: no remote copies, remote signals or barrier semaphores. Data moves between devices by JAX's collectives and lax.ppermute only.
A program may use at most 256 MiB of HBM per device.

v0:
```python
import math

import jax
import jax.numpy as jnp
from jax import lax
from jax.experimental import pallas as pl
from jax.experimental.pallas import tpu as pltpu
from jax.sharding import PartitionSpec as P

BF=jnp.bfloat16; F32=jnp.float32
NEG=-1e30
US = 1150000000
BQ=256
def pair(ref, j, *idx):
    return jnp.concatenate([ref[(2*j,)+idx], ref[(2*j+1,)+idx]], axis=-1)
def dot(a,b):
    return jnp.dot(a,b,preferred_element_type=F32)
def in_range(i, start, end):
    kpos = i*BQ + lax.broadcasted_iota(jnp.int32,(BQ,BQ),0)
    return (kpos>=start)&(kpos<end)
SEG = 384
GROWS = 416


def at(r, w):
    return pl.ds(pl.multiple_of((r * 3 + w) * 64, 64), 64)


def three(bounds_ref, r, j, make, carry):
    lo=bounds_ref[r,j,0]; f0=bounds_ref[r,j,1]; f1=bounds_ref[r,j,2]; hi=bounds_ref[r,j,3]
    carry=lax.fori_loop(lo,f0,make(True),carry)
    carry=lax.fori_loop(f0,f1,make(False),carry)
    return lax.fori_loop(f1,hi,make(True),carry)

def segment_tables(qkv_ref, bounds_ref, se_ref):
    nb = se_ref.shape[1]
    total = nb * BQ
    for r in range(2):
        rows = [qkv_ref[s, SEG : SEG + 16, :].astype(F32)[r : r + 1] for s in range(2 * nb)]
        seg = jnp.concatenate(rows, axis=0)
        edge = [jnp.int32(0)] + [jnp.sum(jnp.where(seg < s, 1.0, 0.0)).astype(jnp.int32) for s in range(1, 6)]
        edge.append(jnp.int32(total))

        def first_of(p):
            v = edge[0]
            for e in edge[1:]:
                v = jnp.where(e <= p, jnp.maximum(v, e), v)
            return v

        def end_of(p):
            v = edge[-1]
            for e in edge[:-1]:
                v = jnp.where(e > p, jnp.minimum(v, e), v)
            return v

        for j in range(nb):
            p0, p1 = j * BQ, j * BQ + BQ - 1
            lo = first_of(p0) // BQ
            hi = (end_of(p1) + BQ - 1) // BQ
            f0 = jnp.clip((first_of(p1) + BQ - 1) // BQ, lo, hi)
            f1 = jnp.clip(end_of(p0) // BQ, f0, hi)
            for i, v in enumerate((lo, f0, f1, hi)):
                bounds_ref[r, j, i] = v
            here = jnp.concatenate([rows[2 * j], rows[2 * j + 1]], axis=-1)
            start = jnp.zeros((1, BQ), jnp.int32)
            end = jnp.full((1, BQ), edge[1], jnp.int32)
            for s in range(1, 6):
                start = jnp.where(here >= s, edge[s], start)
                end = jnp.where(here >= s, edge[s + 1], end)
            se_ref[r, j, 0] = start
            se_ref[r, j, 1] = end


def fwd_kernel(qkv_ref, o_ref, lse_ref, bounds_ref, se_ref, krow, sref):
    nb=krow.shape[1]
    segment_tables(qkv_ref, bounds_ref, se_ref)
    def rows(r, _):
        def tr(i,_):
            krow[r,i]=pair(qkv_ref,i,at(r,1)).T
            return 0
        lax.fori_loop(0,nb,tr,0)
        def qblock(j,_):
            qT=pair(qkv_ref,j,at(r,0))
            start=se_ref[r,j,0]; end=se_ref[r,j,1]
            def p1(masked):
                def body(i,m8):
                    s=dot(krow[r,i],qT)
                    if masked: s=jnp.where(in_range(i,start,end),s,NEG)
                    sref[i]=s
                    return jnp.maximum(m8, jnp.max(s.reshape(BQ//8,8,BQ),axis=0))
                return body
            m8=three(bounds_ref,r,j,p1,jnp.full((8,BQ),NEG,F32))
            m=jnp.max(m8,axis=0,keepdims=True)
            def p2(i,c):
                l8,acc=c
                p=jnp.exp(sref[i]-m)
                l8=l8+jnp.sum(p.reshape(BQ//8,8,BQ),axis=0)
                acc=acc+dot(pair(qkv_ref,i,at(r,2)),p.astype(BF))
                return l8,acc
            l8,acc=lax.fori_loop(bounds_ref[r,j,0],bounds_ref[r,j,3],p2,(jnp.zeros((8,BQ),F32),jnp.zeros((64,BQ),F32)))
            l=jnp.sum(l8,axis=0,keepdims=True)
            o=(acc*(1.0/l)).astype(BF)
            o_ref[2*j,r]=o[:,:128]; o_ref[2*j+1,r]=o[:,128:]
            lse_ref[r,j]=m+jnp.log(l)
            return 0
        lax.fori_loop(0,nb,qblock,0)
        return 0
    lax.fori_loop(0,2,rows,0)

def attn_fwd(qkv):
    ns=qkv.shape[0]; nb=ns//2
    vm=pl.BlockSpec(memory_space=pltpu.VMEM)
    return pl.pallas_call(fwd_kernel,
        in_specs=[vm], out_specs=[vm,vm,pl.BlockSpec(memory_space=pltpu.SMEM),vm],
        out_shape=[jax.ShapeDtypeStruct((ns,2,64,128),BF), jax.ShapeDtypeStruct((2,nb,1,BQ),F32),
                   jax.ShapeDtypeStruct((2,nb,4),jnp.int32), jax.ShapeDtypeStruct((2,nb,2,1,BQ),jnp.int32)],
        scratch_shapes=[pltpu.VMEM((2,nb,BQ,64),BF), pltpu.VMEM((nb,BQ,BQ),F32)],
        compiler_params=pltpu.CompilerParams(vmem_limit_bytes=32<<20),
        cost_estimate=pl.CostEstimate(flops=33 * US,bytes_accessed=3<<20,transcendentals=8<<20),
        name="attn_fwd")(qkv)

def bwd_kernel(bounds_ref, qkv_ref, se_ref, o_ref, g_ref, lse_ref, cs_ref, out_ref, kv, qg, dq, delta):
    nb=kv.shape[0]
    def back(x, i):
        c=pair(cs_ref,i,0); s=pair(cs_ref,i,1)
        a,b=x[:32],x[32:]
        return jnp.concatenate([a*c+b*s, b*c-a*s],axis=0).astype(BF)
    def put(i,r,w,x):
        out_ref[2*i,at(r,w),:]=x[:,:128]; out_ref[2*i+1,at(r,w),:]=x[:,128:]
    def rows(r,_):
        def prep(i,_):
            kT=pair(qkv_ref,i,at(r,1)); vT=pair(qkv_ref,i,at(r,2)); qT=pair(qkv_ref,i,at(r,0)); gT=pair(g_ref,i,pl.ds(pl.multiple_of(r*64,64),64))
            kv[i]=jnp.concatenate([kT,vT],axis=0).T
            qg[i]=jnp.concatenate([qT,gT],axis=0).T
            delta[i]=jnp.sum(gT.astype(F32)*pair(o_ref,i,r).astype(F32),axis=0,keepdims=True)
            dq[i]=jnp.zeros((64,BQ),F32)
            return 0
        lax.fori_loop(0,nb,prep,0)
        lane=lax.broadcasted_iota(jnp.int32,(BQ,128),1)
        def kblock(i,_):
            kvi=kv[i]
            kT=pair(qkv_ref,i,at(r,1))
            z=jnp.zeros((64,BQ),BF)
            def make(masked):
                def body(j,c):
                    dk,dv=c
                    qT=pair(qkv_ref,j,at(r,0)); gT=pair(g_ref,j,pl.ds(pl.multiple_of(r*64,64),64))
                    s=dot(kvi,jnp.concatenate([qT,z],axis=0))
                    p=jnp.exp(s-lse_ref[r,j])
                    if masked: p=jnp.where(in_range(i,se_ref[r,j,0],se_ref[r,j,1]),p,0.0)
                    dp=dot(kvi,jnp.concatenate([z,gT],axis=0))
                    ds=(p*(dp-delta[j])).astype(BF)
                    dv=dv+dot(p.astype(BF),qg[j])
                    dk=dk+dot(ds,qg[j])
                    dq[j]=dq[j]+dot(kT,ds)
                    return dk,dv
                return body
            zz=jnp.zeros((BQ,128),F32)
            dk,dv=three(bounds_ref,r,i,make,(zz,zz))
            dkv=jnp.where(lane<64,dk,dv).T
            put(i,r,1,back(dkv[:64],i))
            put(i,r,2,dkv[64:].astype(BF))
            return 0
        lax.fori_loop(0,nb,kblock,0)
        def fin(i,_):
            put(i,r,0,back(dq[i]*0.125,i))
            return 0
        lax.fori_loop(0,nb,fin,0)
        return 0
    lax.fori_loop(0,2,rows,0)

def attn_bwd(bounds, qkv, se, o, g, lse, cs):
    nb=bounds.shape[1]; ns=qkv.shape[0]
    vm=pl.BlockSpec(memory_space=pltpu.VMEM)
    return pl.pallas_call(bwd_kernel,
        in_specs=[pl.BlockSpec(memory_space=pltpu.SMEM)]+[vm]*6, out_specs=vm,
        out_shape=jax.ShapeDtypeStruct((ns,GROWS,128),BF),
        scratch_shapes=[pltpu.VMEM((nb,BQ,128),BF), pltpu.VMEM((nb,BQ,128),BF), pltpu.VMEM((nb,64,BQ),F32), pltpu.VMEM((nb,1,BQ),F32)],
        compiler_params=pltpu.CompilerParams(vmem_limit_bytes=32<<20),
        cost_estimate=pl.CostEstimate(flops=40 * US,bytes_accessed=6<<20,transcendentals=8<<20),
        name="attn_bwd")(bounds,qkv,se,o,g,lse,cs)


HEADS = 16
HD = 64
D = 1024
FF = 2048
NB = 8
NK = 16
EPS = 1e-06
FR = 128
FC = 512
RT = 32


def nt(a, b):
    return lax.dot_general(a, b, (((1,), (1,)), ((), ())), preferred_element_type=F32)


def normed(x):
    center = x - jnp.mean(x, axis=-1, keepdims=True)
    inv = lax.rsqrt(jnp.mean(center * center, axis=-1, keepdims=True) + EPS)
    return center * inv, inv


def fold(x):
    return jnp.sum(x.reshape(x.shape[0] // 8, 8, x.shape[1]), axis=0)


def row_tiles(body):
    for r in range(2):

        def step(t, _, r=r):
            body(r, pl.ds(pl.multiple_of(r * FR + t * RT, RT), RT))
            return 0

        lax.fori_loop(0, FR // RT, step, 0)


def pre_kernel(x_ref, mod_ref, wq_ref, wk_ref, wv_ref, bq_ref, bk_ref, bv_ref, cs_ref, seg_ref, send_ref, n1_ref, h1):
    @pl.when(pl.program_id(0) == 0)
    def _():
        def body(r, rows):
            n, _ = normed(x_ref[rows, :].astype(F32))
            n1_ref[rows, :] = n.astype(BF)
            h1[rows, :] = (n * (1.0 + mod_ref[r : r + 1, D:]) + mod_ref[r : r + 1, :D]).astype(BF)

        row_tiles(body)

    c = jnp.concatenate([cs_ref[0], cs_ref[0]], axis=-1)
    s = jnp.concatenate([cs_ref[1], cs_ref[1]], axis=-1)
    for w, (w_ref, b_ref) in enumerate(((wq_ref, bq_ref), (wk_ref, bk_ref), (wv_ref, bv_ref))):
        p = (dot(h1[...], w_ref[...]) + b_ref[...].astype(F32)).T
        for h in range(4):
            y = p[h * HD : (h + 1) * HD]
            if w < 2:
                a, b = y[:32], y[32:]
                y = jnp.concatenate([a * c - b * s, b * c + a * s], axis=0)
                if w == 0:
                    y = y * 0.125
            y = y.astype(BF)
            send_ref[h, w * HD : (w + 1) * HD, :] = y[:, :FR]
            send_ref[h, (3 + w) * HD : (4 + w) * HD, :] = y[:, FR:]
    tile = jnp.concatenate([seg_ref[...].astype(F32), jnp.zeros((14, FR), F32)], axis=0).astype(BF)
    for h in range(4):
        send_ref[h, SEG:, :] = tile


def pre(x, mod1, w_qkv, b_qkv, cs_me, segments):
    whole = lambda shape: pl.BlockSpec(shape, lambda g: (0,) * len(shape))
    wb = [pl.BlockSpec((D, 256), lambda g, w=w: (0, 4 * w + g)) for w in range(3)]
    bb = [pl.BlockSpec((1, 256), lambda g, w=w: (0, 4 * w + g)) for w in range(3)]
    return pl.pallas_call(
        pre_kernel,
        grid=(4,),
        in_specs=[whole((256, D)), whole((2, 2 * D))] + wb + bb + [whole((2, 32, FR)), whole((2, FR))],
        out_specs=[pl.BlockSpec((4, SEG + 16, FR), lambda g: (g, 0, 0)), whole((256, D))],
        out_shape=[jax.ShapeDtypeStruct((HEADS, SEG + 16, FR), BF), jax.ShapeDtypeStruct((256, D), BF)],
        scratch_shapes=[pltpu.VMEM((256, D), BF)],
        compiler_params=pltpu.CompilerParams(vmem_limit_bytes=60 << 20),
        cost_estimate=pl.CostEstimate(flops=8 * US, bytes_accessed=9 << 20, transcendentals=0),
        name="pre",
    )(x, mod1, w_qkv, w_qkv, w_qkv, b_qkv, b_qkv, b_qkv, cs_me, segments)


def mid_kernel(
    core_ref, oT_ref, x_ref, cot_ref, mod_ref, bo_ref, bu_ref, bd_ref, wo_hbm, wu_hbm, wd_hbm,
    out_ref, gm_ref, go_ref, a_ref, keep_ref, send_ref,
    wo, wu, wd, b1, mdl, n2, iv, b2, gh2, gb, sums, bsum, sem,
):
    copies = [pltpu.make_async_copy(wo_hbm, wo, sem.at[0])]
    for f in range(4):
        copies.append(pltpu.make_async_copy(wu_hbm.at[:, pl.ds(f * FC, FC)], wu.at[f], sem.at[1 + f]))
        copies.append(pltpu.make_async_copy(wd_hbm.at[pl.ds(f * FC, FC), :], wd.at[f], sem.at[5 + f]))
    for copy in copies:
        copy.start()
    low = core_ref[0] == 0

    def divide(rows, at, g):
        w = g.shape[1] // 2
        a, b = g[:, :w], g[:, w:]
        keep_ref[rows, at : at + w] = jnp.where(low, a, b)
        send_ref[rows, at : at + w] = jnp.where(low, b, a)

    sums[...] = jnp.zeros_like(sums)
    bsum[...] = jnp.zeros_like(bsum)
    o = jnp.concatenate([oT_ref[:, r].reshape(D, FR).T for r in range(2)], axis=0)
    a_ref[:, :D] = o
    copies[0].wait()
    b1[...] = dot(o, wo[...])

    def first(r, rows):
        gate1, shift2 = mod_ref[r : r + 1, :D], mod_ref[r : r + 1, D : 2 * D]
        scale2, gate2 = mod_ref[r : r + 1, 2 * D : 3 * D], mod_ref[r : r + 1, 3 * D :]
        branch = b1[rows, :] + bo_ref[...].astype(F32)
        b1[rows, :] = branch
        middle = x_ref[rows, :].astype(F32) + gate1 * branch
        mdl[rows, :] = middle
        n, inv = normed(middle)
        n2[rows, :] = n
        iv[rows, :] = jnp.broadcast_to(inv, (RT, FR))
        a_ref[rows, D : 2 * D] = (n * (1.0 + scale2) + shift2).astype(BF)
        g = (gate2 * cot_ref[rows, :].astype(F32)).astype(BF)
        gb[rows, :] = g
        divide(rows, 3 * FC, g)
        bsum[:, 3 * D :] += fold(g.astype(F32))

    row_tiles(first)
    for f in range(4):
        copies[1 + 2 * f].wait()
        copies[2 + 2 * f].wait()
        u = dot(a_ref[:, D : 2 * D], wu[f]) + bu_ref[:, f * FC : (f + 1) * FC].astype(F32)
        k = math.sqrt(2.0 / math.pi)
        sq = u * u
        t = jnp.tanh(u * (k + (k * 0.044715) * sq))
        half = 0.5 * (1.0 + t)
        a = (u * half).astype(BF)
        a_ref[:, 2 * D + f * FC : 2 * D + (f + 1) * FC] = a
        slope = half + (0.5 * u) * (1.0 - t * t) * (k + (3.0 * k * 0.044715) * sq)
        gu = (nt(gb[...], wd[f]) * slope).astype(BF)
        at = FC + (f % 2) * FC

        @pl.when(low == (f < 2))
        def _(gu=gu, at=at):
            keep_ref[:, at : at + FC] = gu

        @pl.when(low != (f < 2))
        def _(gu=gu, at=at):
            send_ref[:, at : at + FC] = gu

        bsum[:, D + f * FC : D + (f + 1) * FC] += fold(gu.astype(F32))
        if f == 0:
            b2[...] = dot(a, wd[f])
            gh2[...] = nt(gu, wu[f])
        else:
            b2[...] += dot(a, wd[f])
            gh2[...] += nt(gu, wu[f])

    def last(r, rows):
        gate1, scale2, gate2 = mod_ref[r : r + 1, :D], mod_ref[r : r + 1, 2 * D : 3 * D], mod_ref[r : r + 1, 3 * D :]
        branch = b2[rows, :] + bd_ref[...].astype(F32)
        cot = cot_ref[rows, :].astype(F32)
        out_ref[rows, :] = (mdl[rows, :] + gate2 * branch).astype(BF)
        sums[r, :, 3 * D :] += fold(branch * cot)
        gh, n = gh2[rows, :], n2[rows, :]
        sums[r, :, D : 2 * D] += fold(gh)
        sums[r, :, 2 * D : 3 * D] += fold(gh * n)
        g = gh * (1.0 + scale2)
        back = g - jnp.mean(g, axis=-1, keepdims=True) - n * jnp.mean(g * n, axis=-1, keepdims=True)
        gm = cot + iv[rows, :1] * back
        gm_ref[rows, :] = gm
        sums[r, :, :D] += fold(b1[rows, :] * gm)
        g1 = (gate1 * gm).astype(BF)
        gb[rows, :] = g1
        divide(rows, 0, g1)
        bsum[:, :D] += fold(g1.astype(F32))

    row_tiles(last)
    goT = nt(wo[...], gb[...]).astype(BF)
    part = [jnp.sum(sums[r], axis=0, keepdims=True) for r in range(2)]
    bias = jnp.sum(bsum[...], axis=0, keepdims=True)
    for k in range(NK):
        go_ref[k, 0:HD] = goT[k * HD : (k + 1) * HD, :FR]
        go_ref[k, HD : 2 * HD] = goT[k * HD : (k + 1) * HD, FR:]
        at = lambda v, i: v[:, (2 * k + i) * FR : (2 * k + i + 1) * FR]
        tile = [at(part[0], 0), at(part[0], 1), at(part[1], 0), at(part[1], 1), at(bias, 0), at(bias, 1)]
        go_ref[k, 2 * HD :] = jnp.concatenate(tile + [jnp.zeros((10, FR), F32)], axis=0).astype(BF)


def mid(core, oT, x, cot, mod2, b_out, b_up, b_down, w_out, w_up, w_down):
    vm = pl.BlockSpec(memory_space=pltpu.VMEM)
    hbm = pl.BlockSpec(memory_space=pl.ANY)
    S = jax.ShapeDtypeStruct
    V = pltpu.VMEM
    return pl.pallas_call(
        mid_kernel,
        in_specs=[pl.BlockSpec(memory_space=pltpu.SMEM)] + [vm] * 7 + [hbm] * 3,
        out_specs=[vm] * 6,
        out_shape=[
            S((256, D), BF), S((256, D), F32), S((NK, 144, FR), BF), S((256, 4 * D), BF),
            S((256, 2 * D), BF), S((256, 2 * D), BF),
        ],
        scratch_shapes=[
            V((D, D), BF), V((4, D, FC), BF), V((4, FC, D), BF), V((256, D), F32), V((256, D), F32),
            V((256, D), F32), V((256, FR), F32), V((256, D), F32), V((256, D), F32), V((256, D), BF),
            V((2, 8, 4 * D), F32), V((8, 4 * D), F32), pltpu.SemaphoreType.DMA((9,)),
        ],
        compiler_params=pltpu.CompilerParams(vmem_limit_bytes=48 << 20),
        cost_estimate=pl.CostEstimate(flops=13 * US, bytes_accessed=16 << 20, transcendentals=256 * FF),
        name="mid",
    )(core, oT, x, cot, mod2, b_out, b_up, b_down, w_out, w_up, w_down)


def dw_kernel(oa, ob, ha, hb, aa, ab, ga, gb, out_ref):
    both = lambda a, b: jnp.concatenate([a[...].T, b[...].T], axis=-1)
    frames = lambda i, j: jnp.concatenate([ga[:, i:j], gb[:, i:j]], axis=0)
    out = dot(both(oa, ob), frames(0, FC)).reshape(NK, 8, FC)
    up = dot(both(ha, hb), frames(FC, 3 * FC)).reshape(NK, 8, 2 * FC)
    down = dot(both(aa, ab), frames(3 * FC, 4 * FC)).reshape(NK, 16, FC)
    out_ref[0, :, :, :FC] = down.astype(BF)
    out_ref[0, :, :, FC : 2 * FC] = jnp.concatenate([out, up[..., :FC]], axis=1).astype(BF)
    half = FC // 2
    out_ref[0, :, :, 2 * FC :] = jnp.concatenate([up[..., FC : FC + half], up[..., FC + half :]], axis=1).astype(BF)


def dw(a, a2, g, g2):
    cols = lambda n, first: pl.BlockSpec((256, n), lambda b: (0, first + b))
    whole = pl.BlockSpec((256, 2 * D), lambda b: (0, 0))
    return pl.pallas_call(
        dw_kernel,
        grid=(NB,),
        in_specs=[cols(128, 0)] * 2 + [cols(128, 8)] * 2 + [cols(256, 8)] * 2 + [whole] * 2,
        out_specs=pl.BlockSpec((1, NK, 16, 1280), lambda b: ((b % 4) * 2 + b // 4, 0, 0, 0)),
        out_shape=jax.ShapeDtypeStruct((NB, NK, 16, 1280), BF),
        compiler_params=pltpu.CompilerParams(vmem_limit_bytes=60 << 20),
        cost_estimate=pl.CostEstimate(flops=6 * US, bytes_accessed=12 << 20, transcendentals=0),
        name="dw",
    )(a, a2, a, a2, a, a2, g, g2)


def tail_kernel(g_ref, w_ref, x_ref, gm_ref, mod_ref, out_ref, gh1):
    step = pl.program_id(0)
    acc = None
    for w in range(3):
        g = jnp.concatenate([g_ref[:, (3 * r + w) * HD : (3 * r + w + 1) * HD, :].reshape(D, FR) for r in range(2)], axis=-1)
        t = dot(w_ref[:, w * D : (w + 1) * D], g)
        acc = t if acc is None else acc + t
    gh1[step] = acc.T

    @pl.when(step == pl.num_programs(0) - 1)
    def _():
        def body(r, rows):
            n, inv = normed(x_ref[rows, :].astype(F32))
            g = jnp.concatenate([gh1[i, rows, :] for i in range(4)], axis=-1)
            g = g * (1.0 + mod_ref[r : r + 1, D:])
            back = g - jnp.mean(g, axis=-1, keepdims=True) - n * jnp.mean(g * n, axis=-1, keepdims=True)
            out_ref[rows, :] = gm_ref[rows, :] + inv * back

        row_tiles(body)


def tail(g_back, w_qkv, x, gm, mod1):
    whole = lambda shape: pl.BlockSpec(shape, lambda g: (0,) * len(shape))
    return pl.pallas_call(
        tail_kernel,
        grid=(4,),
        in_specs=[
            whole((HEADS, GROWS, FR)), pl.BlockSpec((256, 3 * D), lambda g: (g, 0)),
            whole((256, D)), whole((256, D)), whole((2, 2 * D)),
        ],
        out_specs=whole((256, D)),
        out_shape=jax.ShapeDtypeStruct((256, D), F32),
        scratch_shapes=[pltpu.VMEM((4, 256, 256), F32)],
        compiler_params=pltpu.CompilerParams(vmem_limit_bytes=60 << 20),
        cost_estimate=pl.CostEstimate(flops=8 * US, bytes_accessed=10 << 20, transcendentals=0),
        name="tail",
    )(g_back, w_qkv, x, gm, mod1)


def wgrad_kernel(blk_ref, g_ref, n_ref, wq_ref, wk_ref, wv_ref, mod_ref, te_ref, gout_ref, gw_ref, s_ref, acc, sacc):
    s = pl.program_id(0)

    @pl.when(s == 0)
    def _():
        acc[...] = jnp.zeros_like(acc)
        sacc[...] = jnp.zeros_like(sacc)

    for r in range(2):
        gt = jnp.concatenate([g_ref[i, r * 192 : (r + 1) * 192, :] for i in range(2)], axis=-1)
        nn = jnp.concatenate([n_ref[i, r * FR : (r + 1) * FR, :] for i in range(2)], axis=0)
        acc[r] += dot(gt, nn)
        sacc[r] += jnp.sum(gt.astype(F32), axis=1, keepdims=True)

    @pl.when(s == pl.num_programs(0) - 1)
    def _():
        even = blk_ref[0] % 2 == 0
        ws = []
        for ref in (wq_ref, wk_ref, wv_ref):
            t = ref[...].astype(F32).T
            ws.append(jnp.where(even, t[:HD], t[HD:]))
        w = jnp.concatenate(ws, axis=0)
        total = jnp.zeros_like(w)
        rows = []
        for r in range(2):
            m, sv = acc[r], sacc[r]
            shift, scale = mod_ref[r : r + 1, :D], mod_ref[r : r + 1, D:]
            total += m * (1.0 + scale) + sv * shift
            rows.append(jnp.concatenate([jnp.sum(w * sv, axis=0, keepdims=True), jnp.sum(w * m, axis=0, keepdims=True)], axis=-1))
        gw_ref[...] = total.T.astype(BF)
        column = jnp.broadcast_to(sacc[0] + sacc[1], (192, FR))
        s_ref[...] = jnp.concatenate([column, jnp.zeros((HD, FR), F32)], axis=0).T[:8]
        for k in range(NK):
            tile = [v[:, k * FR : (k + 1) * FR] for v in rows] + [jnp.zeros((14, FR), F32)]
            gout_ref[k, :16, :] = jnp.concatenate(tile, axis=0).astype(BF)
            gout_ref[k, 16:, :] = te_ref[...]


def wgrad(blk, g, n, w_qkv, mod1, time_early):
    wb = [pl.BlockSpec((D, FR), lambda s, k, w=w: (0, 8 * w + k[0] // 2)) for w in range(3)]
    whole = lambda shape: pl.BlockSpec(shape, lambda s, k: (0,) * len(shape))
    return pl.pallas_call(
        wgrad_kernel,
        grid_spec=pltpu.PrefetchScalarGridSpec(
            num_scalar_prefetch=1,
            grid=(NK // 2,),
            in_specs=[
                pl.BlockSpec((2, SEG, FR), lambda s, k: (s, 0, 0)),
                pl.BlockSpec((2, 256, D), lambda s, k: (s, 0, 0)),
            ] + wb + [whole((2, 2 * D)), whole((16, FR))],
            out_specs=[pl.BlockSpec((NK, 32, FR), lambda s, k: (0, SEG // 32, 0)), whole((D, 192)), whole((8, 256))],
            scratch_shapes=[pltpu.VMEM((2, 192, D), F32), pltpu.VMEM((2, 192, 1), F32)],
        ),
        out_shape=[
            jax.ShapeDtypeStruct((NK, GROWS, FR), BF), jax.ShapeDtypeStruct((D, 192), BF),
            jax.ShapeDtypeStruct((8, 256), F32),
        ],
        input_output_aliases={1: 0},
        compiler_params=pltpu.CompilerParams(vmem_limit_bytes=60 << 20),
        cost_estimate=pl.CostEstimate(flops=9 * US, bytes_accessed=12 << 20, transcendentals=0),
        name="wgrad",
    )(blk, g, n, w_qkv, w_qkv, w_qkv, mod1, time_early)


def a2a(x, axis):
    return lax.all_to_all(x, axis, 0, 0, tiled=True)


def spread(x, axis):
    n = lax.axis_size(axis)
    return a2a(jnp.broadcast_to(x[None], (n,) + x.shape), axis)


def dg(a, b, ca, cb):
    return lax.dot_general(a, b, (((ca,), (cb,)), ((), ())), preferred_element_type=F32)


def to_core(x):
    return lax.ppermute(x, "blk", [(i, i ^ 1) for i in range(NK)])


def after(x, *others):
    return lax.optimization_barrier((x,) + others)[0]


def per_device(
    frames, time_embed, segments, w_mod, b_mod, w_qkv, b_qkv, w_out, b_out,
    w_up, b_up, w_down, b_down, cotangent,
):
    R = frames.shape[0]
    blk = lax.axis_index("blk")
    bat = lax.axis_index("batch")
    core = blk % 2
    me = bat * NK + blk
    x = frames.reshape(R * FR, D)
    time_vals = time_embed.astype(F32)
    time_act, silu_back = jax.vjp(jax.nn.silu, time_vals)
    time_low = time_act.astype(BF)

    def mod_part(a, b):
        return dg(time_low, w_mod[:, a * D : b * D], 1, 0) + b_mod[a * D : b * D].astype(F32)

    mod1 = mod_part(0, 2)
    inverse = jnp.exp(jnp.arange(32, dtype=F32) * (-2.0 * math.log(10000.0) / HD))
    inverse = inverse[:, None]
    mine = (blk * FR + jnp.arange(FR, dtype=jnp.int32)).astype(F32)[None, :]
    cs_me = jnp.stack([jnp.cos(mine * inverse), jnp.sin(mine * inverse)])
    qkv_send, n1 = pre(x, mod1, w_qkv, b_qkv[None], cs_me, segments)
    qkv = a2a(qkv_send, "blk")

    mod2 = mod_part(2, 6)
    pos = jnp.arange(NK * FR, dtype=F32).reshape(NK, 1, FR)
    angles = pos * inverse[None]
    cs = jnp.stack([jnp.cos(angles), jnp.sin(angles)], axis=1)
    w_mod_mine = lax.dynamic_slice_in_dim(w_mod, 2 * D + blk * 256, 256, 1)

    qkv, n1_gather = lax.optimization_barrier((qkv, n1))
    norm_all = lax.all_gather(n1_gather, "blk", axis=0, tiled=False)

    o_heads, lse, bounds, se = attn_fwd(qkv)
    oT = a2a(o_heads, "blk")
    output, g_middle, go_send, a_all, g_keep, g_give = mid(
        core.astype(jnp.int32).reshape(1), oT, x, cotangent.reshape(R * FR, D), mod2, b_out[None], b_up[None], b_down[None], w_out, w_up, w_down
    )
    go = a2a(go_send, "blk")

    a2_all, g2_all = to_core(a_all), to_core(g_give)
    a2_all, g2_all, go, norm_all = lax.optimization_barrier((a2_all, g2_all, go, norm_all))
    dws = dw(a_all, a2_all, g_keep, g2_all)
    x4 = [[4 * y + i for i in range(4)] for y in range(2)]
    dws = lax.psum_scatter(dws.reshape(NB * 256, 1280), "batch", scatter_dimension=0, axis_index_groups=x4, tiled=True)

    early = jnp.sum(go[:, 128:134].astype(F32), axis=0).reshape(3, 256).astype(BF)
    time_early = dg(early[:2], w_mod_mine, 1, 1).astype(BF)

    g_qkvT = attn_bwd(bounds, qkv, se, o_heads, go, lse, cs)
    g_qkvT, gw_qkv, s_rows = wgrad(
        blk.astype(jnp.int32).reshape(1), g_qkvT, norm_all, w_qkv, mod1, time_early.reshape(16, FR)
    )
    dws = after(dws, gw_qkv).reshape(2, NK, 16, 1280)
    g_back = a2a(g_qkvT, "blk")
    tail_mine = jnp.sum(g_back[:, 384:386].astype(F32), axis=0)
    time_early = jnp.sum(g_back[:, 400:416].astype(F32), axis=0).reshape(R, D)

    def rows_of(v, n):
        return jnp.broadcast_to(v.astype(BF).reshape(1, 8, n), (NB * NK, 8, n))

    pack = jnp.concatenate(
        [
            gw_qkv.reshape(NB * NK, 8, 192),
            rows_of(tail_mine, 32),
            rows_of(early, 96),
            rows_of(s_rows[0, :192], 24),
            time_low.reshape(R, NB * NK, 8).transpose(1, 2, 0),
        ],
        axis=-1,
    )
    pack, dws = lax.optimization_barrier((pack, dws))
    dw_got = lax.ppermute(
        lax.dynamic_index_in_dim(dws, 1 - bat // 4, 0, keepdims=False), "batch", [(i, i ^ 4) for i in range(NB)]
    )
    dws = lax.dynamic_index_in_dim(dws, bat // 4, 0, keepdims=False).astype(F32) + dw_got.astype(F32)
    dws = dws.astype(BF)
    g_back = after(g_back, dws)
    got = a2a(pack, ("batch", "blk")).reshape(NB, NK, 8, 346)
    gq = jnp.sum(got[..., :192].astype(F32), axis=0).reshape(NK, 8, 3, HD)
    grad_w_qkv = gq.transpose(1, 2, 0, 3).reshape(8, 3 * D)
    rows_tail = got[..., 192:224].reshape(NB, NK, R, FR).transpose(0, 2, 1, 3).reshape(NB * R, 2 * D)
    vec = got[..., 224:320].reshape(NB, NK, 3, 256)
    rows_early = vec[:, :, :2].transpose(0, 2, 1, 3).reshape(NB * R, 4 * D)
    rows_all = jnp.concatenate([rows_tail, rows_early], axis=1)
    act_mine = got[:, 0, :, 344:].transpose(0, 2, 1).reshape(NB * R, 8)
    grad_w_mod = dg(act_mine, rows_all, 0, 0)
    b_mod_sum = jnp.sum(rows_all.astype(F32), axis=0)
    grad_b_mod = lax.dynamic_slice_in_dim(b_mod_sum, me * 48, 48)
    biases = jnp.sum(vec[:, :, 2].astype(F32), axis=0).reshape(4 * D)
    grad_b_out = lax.dynamic_slice_in_dim(biases, me * 8, 8)
    grad_b_up = lax.dynamic_slice_in_dim(biases, D + me * 16, 16)
    grad_b_down = lax.dynamic_slice_in_dim(biases, 3 * D + me * 8, 8)
    b_qkv_sum = jnp.sum(got[..., 320:344].astype(F32), axis=0).reshape(NK, 3, HD).transpose(1, 0, 2).reshape(3 * D)
    grad_b_qkv = lax.dynamic_slice_in_dim(b_qkv_sum, me * 24, 24)
    rows_mine = lax.dynamic_slice_in_dim(rows_tail, bat * R, R, 0)
    (grad_time,) = silu_back(time_early + dg(rows_mine, w_mod[:, : 2 * D], 1, 1))

    dws = a2a(after(dws, got), "blk").reshape(NK // 2, 2, 16, 1280)
    dws = jnp.sum(dws.astype(F32), axis=0)
    grad_w_down = jnp.concatenate([dws[0, :, :FC], dws[1, :, :FC]], axis=1)
    grad_w_out = jnp.concatenate([dws[0, :8, FC : 2 * FC], dws[1, :8, FC : 2 * FC]], axis=1)
    grad_w_up = jnp.concatenate(
        [v for c in range(2) for v in (dws[c, 8:, FC : 2 * FC], dws[c, :8, 2 * FC :], dws[c, 8:, 2 * FC :])], axis=1
    )

    grad_frames = tail(g_back, w_qkv, x, g_middle, mod1)
    return (
        output.reshape(R, FR, D), grad_frames.reshape(R, FR, D), grad_time, grad_w_mod, grad_b_mod, grad_w_qkv,
        grad_b_qkv, grad_w_out, grad_b_out, grad_w_up, grad_b_up, grad_w_down, grad_b_down,
    )

def solution(mesh):
    both = ("batch", "blk")
    return jax.shard_map(
        per_device,
        mesh=mesh,
        in_specs=(
            P("batch", "blk", None), P("batch", None), P("batch", "blk"),
            P(), P(), P(), P(), P(), P(), P(), P(), P(), P(),
            P("batch", "blk", None),
        ),
        out_specs=(
            P("batch", "blk", None), P("batch", "blk", None), P("batch", None),
            P(both, None), P(both), P(both, None), P(both), P(both, None), P(both),
            P(both, None), P(both), P(both, None), P(both),
        ),
        check_vma=False,
    )
```

profile of v0, /device:TPU:2, one launch (start us, length us, event | category | flops | bytes accessed | tf_op | source)
XLA Modules:
  0.0 307.7 jit_solution(16091493079700031198)
XLA Ops:
  7.9 1.3 broadcast_in_dim.16.bq_ref.bk_ref.bv_ref
  10.0 3.5 %fusion.9.mod_ref = f32[2,2048]{1,0:T(2,128)} fusion(bf16[1024,6144]{1,0:T(8,128)(2,1)} %param.17, f32[2048]{0:T(1024)S(1)} %slice_convert_fusion.2, bf16[2,1024]{1,0:T(2,128)(2,1)} %param.15), kind=kOutput, calls=%fused_computation.7 | convolution fusion | flops 8404992 | bytes 4222976 | tf_op jit(solution)/shard_map/dot_general | solution.py:534
  13.5 8.1 %pre.1 = (bf16[16,400,128]{2,1,0:T(8,128)(2,1)}, bf16[256,1024]{1,0:T(8,128)(2,1)}) custom-call(bf16[256,1024]{1,0:T(8,128)(2,1)} %bitcast.83, f32[2,2048]{1,0:T(2,128)} %fusion.9.mod_ref, bf16[1024,3072]{1,0:T(8,128)(2,1)} %w_ref.1, bf16[1024,3072]{1,0:T(8,128)(2,1)} %w_ref.1, bf16[1024,3072]{1,0:T(8,128)(2,1)} %w_ref.1, ...), custom_call_target="tpu_custom_call" | custom-call | flops 9200000000 | bytes 9437184 | tf_op jit(solution)/shard_map/pre/pallas_call | solution.py:253
  21.6 32.4 %all_to_all.30.qkv_ref = bf16[16,400,128]{2,1,0:T(8,128)(2,1)S(1)} all-to-all(bf16[16,400,128]{2,1,0:T(8,128)(2,1)} %get-tuple-element.39), channel_id=1, replica_groups=mesh['batch'=8,'blk'=16] {'blk'}, dimensions={0} | all-to-all | bytes 3276800 | tf_op jit(solution)/shard_map/all_to_all | solution.py:525
  54.1 36.6 %attn_fwd.1 = (bf16[16,2,64,128]{3,2,1,0:T(8,128)(2,1)}, f32[2,8,1,256]{3,2,1,0:T(1,128)S(1)}, s32[2,8,4]{2,1,0:T(8,128)S(1)}, s32[2,8,2,1,256]{4,3,2,1,0:T(1,128)S(1)}) custom-call(bf16[16,400,128]{2,1,0:T(8,128)(2,1)S(1)} %all_to_all.30.qkv_ref), custom_call_target="tpu_custom_call" | custom-call | flops 37950001152 | bytes 3145728 | tf_op jit(solution)/shard_map/attn_fwd/pallas_call | solution.py:113
  90.7 3.6 %all-to-all-start.1 = ((bf16[16,2,64,128]{3,2,1,0:T(8,128)(2,1)}), bf16[16,2,64,128]{3,2,1,0:T(8,128)(2,1)S(1)}, u32[]{:S(2)}, u32[]{:S(2)}) async-start(bf16[16,2,64,128]{3,2,1,0:T(8,128)(2,1)} %get-tuple-element.42.o_ref), calls=%async_computation.1 | async-start | bytes 1048576 | tf_op jit(solution)/shard_map/all_to_all | solution.py:525
  94.4 4.7 %fusion.2.mod_ref = f32[2,4096]{1,0:T(2,128)S(1)} fusion(bf16[1024,6144]{1,0:T(8,128)(2,1)} %param.17, f32[4096]{0:T(1024)S(1)} %slice_convert_fusion.1, bf16[2,1024]{1,0:T(2,128)(2,1)S(1)} %copy-done.7), kind=kOutput, calls=%fused_computation.2 | convolution fusion | flops 16797696 | bytes 8441856 | tf_op jit(solution)/shard_map/dot_general | solution.py:534
  99.1 13.5 %all-to-all-done.1.oT_ref = bf16[16,2,64,128]{3,2,1,0:T(8,128)(2,1)S(1)} async-done(((bf16[16,2,64,128]{3,2,1,0:T(8,128)(2,1)}), bf16[16,2,64,128]{3,2,1,0:T(8,128)(2,1)S(1)}, u32[]{:S(2)}, u32[]{:S(2)}) %all-to-all-start.1) | async-done | bytes 524320 | tf_op jit(solution)/shard_map/all_to_all | solution.py:525
  112.6 13.4 %mid.1 = (bf16[256,1024]{1,0:T(8,128)(2,1)}, f32[256,1024]{1,0:T(8,128)S(1)}, bf16[16,144,128]{2,1,0:T(8,128)(2,1)S(1)}, bf16[256,4096]{1,0:T(8,128)(2,1)}, bf16...) custom-call(s32[1]{0:T(128)} %bitcast.core_ref, bf16[16,2,64,128]{3,2,1,0:T(8,128)(2,1)S(1)} %all-to-all-done.1.oT_ref, ...), custom_call_target="tpu_custom_call" | custom-call | flops 14949999616 | bytes 16777216 | tf_op jit(solution)/shard_map/mid/pallas_call | solution.py:375
  127.5 15.8 %all_to_all.31.g_ref = bf16[16,144,128]{2,1,0:T(8,128)(2,1)S(1)} all-to-all(bf16[16,144,128]{2,1,0:T(8,128)(2,1)S(1)} %get-tuple-element.48), channel_id=1, replica_groups=mesh['batch'=8,'blk'=16] {'blk'}, dimensions={0} | all-to-all | bytes 1179648 | tf_op jit(solution)/shard_map/all_to_all | solution.py:525
  144.3 9.7 %dw.1 = bf16[8,16,16,1280]{3,2,1,0:T(8,128)(2,1)} custom-call(bf16[256,4096]{1,0:T(8,128)(2,1)} %get-tuple-element.46.oa.ha.aa, bf16[256,4096]{1,0:T(8,128)(2,1)} %collective-permute-done.ob.hb.ab, bf16[256,4096]{1,0:T(8,128)(2,1)} %get-tuple-element.46.oa.ha.aa, bf16[256,4096]{1,0:T(8,128)(2,1)} %collective-permute-done.ob.hb.ab, ...), custom_call_target="tpu_custom_call" | custom-call | flops 6899999744 | bytes 12582912 | tf_op jit(solution)/shard_map/dw/pallas_call | solution.py:409
  157.0 42.1 %attn_bwd.1.g_ref = bf16[16,416,128]{2,1,0:T(8,128)(2,1)S(1)} custom-call(s32[2,8,4]{2,1,0:T(8,128)S(1)} %get-tuple-element.44.bounds_ref, bf16[16,400,128]{2,1,0:T(8,128)(2,1)S(1)} %all_to_all.30.qkv_ref, s32[2,8,2,1,256]{4,3,2,1,0:T(1,128)S(1)} %get-tuple-element.45.se_ref, bf16[16,2,64,128]{3,2,1,0:T(8,128)(2,1)} %get-tuple-element.42.o_ref, ...), custom_call_target="tpu_custom_call" | custom-call | flops 46000001024 | bytes 6291456 | tf_op jit(solution)/shard_map/attn_bwd/pallas_call | solution.py:175
  200.3 9.6 %wgrad.1 = (bf16[16,416,128]{2,1,0:T(8,128)(2,1)}, bf16[1024,192]{1,0:T(8,128)(2,1)}, f32[8,256]{1,0:T(8,128)}) custom-call(s32[1]{0:T(128)} %bitcast.4.blk_ref, bf16[16,416,128]{2,1,0:T(8,128)(2,1)} %copy-done, bf16[16,256,1024]{2,1,0:T(8,128)(2,1)} %bitcast.109, bf16[1024,3072]{1,0:T(8,128)(2,1)} %w_ref.1, ...), custom_call_target="tpu_custom_call", output_to_operand_aliasing={{0}: (1, {})} | custom-call | flops 10350000128 | bytes 12582912 | tf_op jit(solution)/shard_map/wgrad/pallas_call | solution.py:501
  210.0 3.8 %all-to-all-start.3 = ((bf16[16,416,128]{2,1,0:T(8,128)(2,1)}), bf16[16,416,128]{2,1,0:T(8,128)(2,1)S(1)}, u32[]{:S(2)}, u32[]{:S(2)}) async-start(bf16[16,416,128]{2,1,0:T(8,128)(2,1)} %get-tuple-element.53), calls=%async_computation.3 | async-start | bytes 3407872 | tf_op jit(solution)/shard_map/all_to_all | solution.py:525
  215.7 23.2 %all-to-all-done.3.g_ref = bf16[16,416,128]{2,1,0:T(8,128)(2,1)S(1)} async-done(((bf16[16,416,128]{2,1,0:T(8,128)(2,1)}), bf16[16,416,128]{2,1,0:T(8,128)(2,1)S(1)}, u32[]{:S(2)}, u32[]{:S(2)}) %all-to-all-start.3) | async-done | bytes 1703968 | tf_op jit(solution)/shard_map/all_to_all | solution.py:525
  239.1 2.9 concatenate.15
  242.1 2.0 dynamic-slice_bitcast_fusion
  244.1 6.2 %all-to-all-start.4 = ((bf16[128,8,346]{2,1,0:T(8,128)(2,1)}), bf16[128,8,346]{2,1,0:T(8,128)(2,1)S(1)}, u32[]{:S(2)}, u32[]{:S(2)}) async-start(bf16[128,8,346]{2,1,0:T(8,128)(2,1)} %concatenate.15), calls=%async_computation.5 | async-start | bytes 1572864 | tf_op jit(solution)/shard_map/all_to_all | solution.py:525
  250.3 17.5 %collective-permute-done.2 = bf16[16,16,1280]{2,1,0:T(8,128)(2,1)S(1)} collective-permute-done((bf16[16,16,1280]{2,1,0:T(8,128)(2,1)}, bf16[16,16,1280]{2,1,0:T(8,128)(2,1)S(1)}, u32[]{:S(2)}, u32[]{:S(2)}) %collective-permute-start.2) | collective-permute-done | bytes 655392 | tf_op jit(solution)/shard_map/ppermute | solution.py:618
  267.8 2.1 fusion.12
  269.9 9.1 %tail.1 = f32[256,1024]{1,0:T(8,128)} custom-call(bf16[16,416,128]{2,1,0:T(8,128)(2,1)} %copy-done.5, bf16[1024,3072]{1,0:T(8,128)(2,1)} %w_ref.1, bf16[256,1024]{1,0:T(8,128)(2,1)} %bitcast.84, f32[256,1024]{1,0:T(8,128)} %copy-done.4, f32[2,2048]{1,0:T(2,128)} %fusion.9.mod_ref), custom_call_target="tpu_custom_call" | custom-call | flops 9200000000 | bytes 10485760 | tf_op jit(solution)/shard_map/tail/pallas_call | solution.py:444
  280.7 5.0 %all-to-all-start.5 = ((bf16[16,16,1280]{2,1,0:T(8,128)(2,1)}), bf16[16,16,1280]{2,1,0:T(8,128)(2,1)S(1)}, u32[]{:S(2)}, u32[]{:S(2)}) async-start(bf16[16,16,1280]{2,1,0:T(8,128)(2,1)} %fusion.12), calls=%async_computation.6 | async-start | bytes 1310720 | tf_op jit(solution)/shard_map/all_to_all | solution.py:525
  290.3 4.0 %fusion.23 = f32[2,1024]{1,0:T(2,128)} fusion(bf16[2,1024]{1,0:T(2,128)(2,1)S(1)} %copy-done.7, f32[2,1024]{1,0:T(2,128)S(1)} %reshape.273, bf16[1024,6144]{1,0:T(8,128)(2,1)} %param.17, bf16[16,2048]{1,0:T(8,128)(2,1)S(1)} %bitcast.105, s32[]{:T(128)S(6)} %select_n.45), kind=kOutput, calls=%fused_computation.56 | convolution fusion | flops 8411136 | bytes 4222980 | tf_op jit(solution)/shard_map/dot_general | solution.py:534
  294.3 5.2 %all-to-all-done.5 = bf16[16,16,1280]{2,1,0:T(8,128)(2,1)S(1)} async-done(((bf16[16,16,1280]{2,1,0:T(8,128)(2,1)}), bf16[16,16,1280]{2,1,0:T(8,128)(2,1)S(1)}, u32[]{:S(2)}, u32[]{:S(2)}) %all-to-all-start.5) | async-done | bytes 655392 | tf_op jit(solution)/shard_map/all_to_all | solution.py:525
  (110 shorter events, 17.9 us)
Async XLA Ops:
  7.2 136.2 %all-gather.3.cloned.1.call-start = ((), (), s32[]{:S(2)}) async-start(), calls=%async_computation.8 | async-start | bytes 8912896 | tf_op jit(solution)/shard_map/all_gather | solution.py:577
  13.5 40.5 %copy-start.11 = (bf16[1024]{0:T(1024)(128)(2,1)S(1)}, bf16[1024]{0:T(1024)(128)(2,1)}, u32[]{:S(2)}) copy-start(bf16[1024]{0:T(1024)(128)(2,1)} %param.22) | copy-start | bytes 6148
  13.5 40.5 %copy-start.9 = (bf16[2048]{0:T(1024)(128)(2,1)S(1)}, bf16[2048]{0:T(1024)(128)(2,1)}, u32[]{:S(2)}) copy-start(bf16[2048]{0:T(1024)(128)(2,1)} %param.24) | copy-start | bytes 12292
  13.5 40.6 %copy-start.12 = (bf16[1024]{0:T(1024)(128)(2,1)S(1)}, bf16[1024]{0:T(1024)(128)(2,1)}, u32[]{:S(2)}) copy-start(bf16[1024]{0:T(1024)(128)(2,1)} %param.26) | copy-start | bytes 6148
  13.5 40.6 %copy-start.8 = (bf16[6144]{0:T(1024)(128)(2,1)S(1)}, bf16[6144]{0:T(1024)(128)(2,1)}, u32[]{:S(2)}) copy-start(bf16[6144]{0:T(1024)(128)(2,1)} %param.18) | copy-start | bytes 36868
  54.1 40.3 %copy-start.7 = (bf16[2,1024]{1,0:T(2,128)(2,1)S(1)}, bf16[2,1024]{1,0:T(2,128)(2,1)}, u32[]{:S(2)}) copy-start(bf16[2,1024]{1,0:T(2,128)(2,1)} %param.15) | copy-start | bytes 12292
  90.7 21.9 %all-to-all-start.1 = ((bf16[16,2,64,128]{3,2,1,0:T(8,128)(2,1)}), bf16[16,2,64,128]{3,2,1,0:T(8,128)(2,1)S(1)}, u32[]{:S(2)}, u32[]{:S(2)}) async-start(bf16[16,2,64,128]{3,2,1,0:T(8,128)(2,1)} %get-tuple-element.42.o_ref), calls=%async_computation.1 | async-start | bytes 1048576 | tf_op jit(solution)/shard_map/all_to_all | solution.py:525
  94.3 18.3 %copy-start.1 = (bf16[2,128,1024]{2,1,0:T(8,128)(2,1)S(1)}, bf16[2,128,1024]{2,1,0:T(8,128)(2,1)}, u32[]{:S(2)}) copy-start(bf16[2,128,1024]{2,1,0:T(8,128)(2,1)} %param.27) | copy-start | bytes 1572868
  94.3 18.3 %copy-start.2 = (bf16[2,128,1024]{2,1,0:T(8,128)(2,1)S(1)}, bf16[2,128,1024]{2,1,0:T(8,128)(2,1)}, u32[]{:S(2)}) copy-start(bf16[2,128,1024]{2,1,0:T(8,128)(2,1)} %param.14) | copy-start | bytes 1572868
  94.3 147.7 %reduce-scatter.2.cloned.1.call-start = ((), (), s32[]{:S(2)}) async-start(), calls=%async_computation.7 | async-start | bytes 6553600 | tf_op jit(solution)/shard_map/reduce_scatter | solution.py:590
  125.9 1.0 copy-start.4
  127.0 16.4 %copy-start.3 = (bf16[256,2048]{1,0:T(8,128)(2,1)}, bf16[256,2048]{1,0:T(8,128)(2,1)S(1)}, u32[]{:S(2)}) copy-start(bf16[256,2048]{1,0:T(8,128)(2,1)S(1)} %get-tuple-element.57.ga) | copy-start | bytes 3145732
  127.0 16.4 %collective-permute-start = (bf16[256,4096]{1,0:T(8,128)(2,1)}, bf16[256,4096]{1,0:T(8,128)(2,1)}, u32[]{:S(2)}, u32[]{:S(2)}) collective-permute-start(bf16[256,4096]{1,0:T(8,128)(2,1)} %get-tuple-element.46.oa.ha.aa), channel_id=1, source_target_pairs={{0,1},{1,0},{2,3},{3,2},{4,5},{5,4},{6,7},{7,6},{8,9},{9,8},{10,11... | collective-permute-start | bytes 6291464 | tf_op jit(solution)/shard_map/ppermute | solution.py:538
  127.0 16.3 %collective-permute-start.1 = (bf16[256,2048]{1,0:T(8,128)(2,1)S(1)}, bf16[256,2048]{1,0:T(8,128)(2,1)S(1)}, u32[]{:S(2)}, u32[]{:S(2)}) collective-permute-start(bf16[256,2048]{1,0:T(8,128)(2,1)S(1)} %get-tuple-element.47), channel_id=1, source_target_pairs={{0,1},{1,0},{2,3},{3,2},{4,5},{5,4},{6,7},{7,6},{8,9},{9,8},{10,11... | collective-permute-start | bytes 3145736 | tf_op jit(solution)/shard_map/ppermute | solution.py:538
  143.3 1.0 copy-start.13
  199.1 1.2 copy-start
  210.0 29.2 %copy-start.6 = (bf16[1024,192]{1,0:T(8,128)(2,1)S(1)}, bf16[1024,192]{1,0:T(8,128)(2,1)}, u32[]{:S(2)}) copy-start(bf16[1024,192]{1,0:T(8,128)(2,1)} %get-tuple-element.54) | copy-start | bytes 1179652
  210.0 28.9 %all-to-all-start.3 = ((bf16[16,416,128]{2,1,0:T(8,128)(2,1)}), bf16[16,416,128]{2,1,0:T(8,128)(2,1)S(1)}, u32[]{:S(2)}, u32[]{:S(2)}) async-start(bf16[16,416,128]{2,1,0:T(8,128)(2,1)} %get-tuple-element.53), calls=%async_computation.3 | async-start | bytes 3407872 | tf_op jit(solution)/shard_map/all_to_all | solution.py:525
  238.9 31.0 %copy-start.5 = (bf16[16,416,128]{2,1,0:T(8,128)(2,1)}, bf16[16,416,128]{2,1,0:T(8,128)(2,1)S(1)}, u32[]{:S(2)}) copy-start(bf16[16,416,128]{2,1,0:T(8,128)(2,1)S(1)} %all-to-all-done.3.g_ref) | copy-start | bytes 5111812
  244.0 23.8 %collective-permute-start.2 = (bf16[16,16,1280]{2,1,0:T(8,128)(2,1)}, bf16[16,16,1280]{2,1,0:T(8,128)(2,1)S(1)}, u32[]{:S(2)}, u32[]{:S(2)}) collective-permute-start(bf16[16,16,1280]{2,1,0:T(8,128)(2,1)} %dynamic-slice_bitcast_fusion), channel_id=1, source_target_pairs={{0,64},{16,80},{32,96},{48,112},{64,0},{80,16},{96,32},{112,48},{1... | collective-permute-start | bytes 1966088 | tf_op jit(solution)/shard_map/ppermute | solution.py:618
  244.1 35.0 %all-to-all-start.4 = ((bf16[128,8,346]{2,1,0:T(8,128)(2,1)}), bf16[128,8,346]{2,1,0:T(8,128)(2,1)S(1)}, u32[]{:S(2)}, u32[]{:S(2)}) async-start(bf16[128,8,346]{2,1,0:T(8,128)(2,1)} %concatenate.15), calls=%async_computation.5 | async-start | bytes 1572864 | tf_op jit(solution)/shard_map/all_to_all | solution.py:525
  280.7 18.8 %all-to-all-start.5 = ((bf16[16,16,1280]{2,1,0:T(8,128)(2,1)}), bf16[16,16,1280]{2,1,0:T(8,128)(2,1)S(1)}, u32[]{:S(2)}, u32[]{:S(2)}) async-start(bf16[16,16,1280]{2,1,0:T(8,128)(2,1)} %fusion.12), calls=%async_computation.6 | async-start | bytes 1310720 | tf_op jit(solution)/shard_map/all_to_all | solution.py:525
  299.6 1.3 copy-start.10
Sparse Core Ops, SparseCore 0:
  54.1 79.1 all-gather.2
  154.1 49.6 reduce-scatter.1
where the time goes:
time: 309 us; the launch traced here: 308 us
  Pallas kernels  129 us (42%)
  waiting for transfers between devices  59.4 us (19%)
  blocking collectives  48.2 us (16%)
  starting transfers between devices  19.2 us (6%)
  local copies, waits for them, and re-layouts  16.8 us (5%)
  between operations  14.6 us (5%)
  matrix products  14.3 us (5%)
  other arithmetic  6.51 us (2%)
    all_to_all x2, blocking collectives, a2a(): return lax.all_to_all(x, axis, 0, 0, tiled=True)  48.2 us
    pallas_call x1, Pallas kernels, attn_bwd(): pl.pallas_call(bwd_kernel, in_specs=[pl.BlockSpec(memory_space=pltpu.SMEM...  42.1 us
    all_to_all x4, waiting for transfers between devices, a2a(): return lax.all_to_all(x, axis, 0, 0, tiled=True)  41.8 us
    pallas_call x1, Pallas kernels, attn_fwd(): pl.pallas_call(fwd_kernel, in_specs=[vm], out_specs=[vm, vm, pl.BlockSpec...  36.6 us
    all_to_all x4, starting transfers between devices, a2a(): return lax.all_to_all(x, axis, 0, 0, tiled=True)  18.6 us
    ppermute x1, waiting for transfers between devices, per_device(): lax.ppermute(lax.dynamic_index_in_dim(dws, 1 - bat // 4, 0, keepdims=Fals...  17.5 us
    dot_general x5, matrix products, dg(): lax.dot_general(a, b, (((ca,), (cb,)), ((), ())), preferred_element_type=...  14.3 us
    pallas_call x1, Pallas kernels, mid(): pl.pallas_call(mid_kernel, in_specs=[pl.BlockSpec(memory_space=pltpu.SMEM...  13.4 us
  transfers between devices with their start and end apart: 9, of which 4 were waited for; matrix products, arithmetic and copies ran while one was open for 8% of the time, Pallas kernels for 36%

commit v1 on v0

v1 whole, which is shorter than its diff:
```python
import math

import jax
import jax.numpy as jnp
from jax import lax
from jax.experimental import pallas as pl
from jax.experimental.pallas import tpu as pltpu
from jax.sharding import PartitionSpec as P

BF = jnp.bfloat16
F32 = jnp.float32
NEG = -1e30
US = 1150000000
SEG = 384
GROWS = 416
LN = 128
FQ = FK = 2048
BQ = BK = 512


def dot(a, b):
    return jnp.dot(a, b, preferred_element_type=F32)


def nt(a, b):
    return lax.dot_general(a, b, (((1,), (1,)), ((), ())), preferred_element_type=F32)


def at(r, w):
    return pl.ds(pl.multiple_of((r * 3 + w) * 64, 64), 64)


def lanes(ref, j, n, *idx):
    m = n // LN
    return jnp.concatenate([ref[(j * m + i,) + idx] for i in range(m)], axis=-1)


def first_of(edge_ref, r, p):
    v = jnp.int32(0)
    for i in range(1, 6):
        e = edge_ref[r, i]
        v = jnp.where(e <= p, jnp.maximum(v, e), v)
    return v


def end_of(edge_ref, r, p):
    v = edge_ref[r, 6]
    for i in range(1, 6):
        e = edge_ref[r, i]
        v = jnp.where(e > p, jnp.minimum(v, e), v)
    return v


def over_blocks(edge_ref, r, j, size, step, make, carry):
    p0 = j * size
    p1 = p0 + size - 1
    lo = first_of(edge_ref, r, p0) // step
    hi = (end_of(edge_ref, r, p1) + step - 1) // step
    f0 = jnp.clip((first_of(edge_ref, r, p1) + step - 1) // step, lo, hi)
    f1 = jnp.clip(end_of(edge_ref, r, p0) // step, f0, hi)
    carry = lax.fori_loop(lo, f0, make(True), carry)
    carry = lax.fori_loop(f0, f1, make(False), carry)
    return lax.fori_loop(f1, hi, make(True), carry), lo, hi


def in_range(i, nk, start, end):
    kpos = i * nk + lax.broadcasted_iota(jnp.int32, (nk, start.shape[1]), 0)
    return (kpos >= start) & (kpos < end)


def fold8(x, op):
    return op(x.reshape(x.shape[0] // 8, 8, x.shape[1]), axis=0)


def segment_tables(qkv_ref, edge_ref, se_ref):
    ns = se_ref.shape[1]
    for r in range(2):
        rows = [qkv_ref[s, SEG : SEG + 16, :].astype(F32)[r : r + 1] for s in range(ns)]
        seg = jnp.concatenate(rows, axis=0)
        edge = [jnp.int32(0)] + [jnp.sum(jnp.where(seg < s, 1.0, 0.0)).astype(jnp.int32) for s in range(1, 6)]
        edge.append(jnp.int32(ns * LN))
        for i in range(7):
            edge_ref[r, i] = edge[i]
        edge_ref[r, 7] = jnp.int32(0)
        for s in range(ns):
            start = jnp.zeros((1, LN), jnp.int32)
            end = jnp.full((1, LN), edge[1], jnp.int32)
            for i in range(1, 6):
                start = jnp.where(rows[s] >= i, edge[i], start)
                end = jnp.where(rows[s] >= i, edge[i + 1], end)
            se_ref[r, s, 0:1, :] = start
            se_ref[r, s, 1:2, :] = end


def spans(se_ref, r, j, n):
    m = n // LN
    return [jnp.concatenate([se_ref[r, j * m + i, w : w + 1, :] for i in range(m)], axis=-1) for w in range(2)]


def fwd_kernel(qkv_ref, o_ref, lse_ref, edge_ref, se_ref, krow, sref):
    total = qkv_ref.shape[0] * LN
    segment_tables(qkv_ref, edge_ref, se_ref)

    def rows(r, _):
        def tr(i, _):
            krow[i] = lanes(qkv_ref, i, FK, at(r, 1)).T
            return 0

        lax.fori_loop(0, total // FK, tr, 0)

        def qblock(j, _):
            qT = lanes(qkv_ref, j, FQ, at(r, 0))
            start, end = spans(se_ref, r, j, FQ)

            def make(masked):
                def body(i, m8):
                    s = dot(krow[i], qT)
                    if masked:
                        s = jnp.where(in_range(i, FK, start, end), s, NEG)
                    sref[i] = s
                    return jnp.maximum(m8, fold8(s, jnp.max))

                return body

            m8, lo, hi = over_blocks(edge_ref, r, j, FQ, FK, make, jnp.full((8, FQ), NEG, F32))
            m = jnp.max(m8, axis=0, keepdims=True)

            def second(i, c):
                l8, acc = c
                p = jnp.exp(sref[i] - m)
                return l8 + fold8(p, jnp.sum), acc + dot(lanes(qkv_ref, i, FK, at(r, 2)), p.astype(BF))

            l8, acc = lax.fori_loop(lo, hi, second, (jnp.zeros((8, FQ), F32), jnp.zeros((64, FQ), F32)))
            l = jnp.sum(l8, axis=0, keepdims=True)
            o = (acc * (1.0 / l)).astype(BF)
            lse = m + jnp.log(l)
            for i in range(FQ // LN):
                o_ref[j * (FQ // LN) + i, r] = o[:, i * LN : (i + 1) * LN]
                lse_ref[r, j * (FQ // LN) + i] = jnp.broadcast_to(lse[:, i * LN : (i + 1) * LN], (8, LN))
            return 0

        lax.fori_loop(0, total // FQ, qblock, 0)
        return 0

    lax.fori_loop(0, 2, rows, 0)


def attn_fwd(qkv):
    ns = qkv.shape[0]
    vm = pl.BlockSpec(memory_space=pltpu.VMEM)
    S = jax.ShapeDtypeStruct
    return pl.pallas_call(
        fwd_kernel,
        in_specs=[vm],
        out_specs=[vm, vm, pl.BlockSpec(memory_space=pltpu.SMEM), vm],
        out_shape=[S((ns, 2, 64, LN), BF), S((2, ns, 8, LN), F32), S((2, 8), jnp.int32), S((2, ns, 8, LN), jnp.int32)],
        scratch_shapes=[pltpu.VMEM((ns * LN // FK, FK, 64), BF), pltpu.VMEM((ns * LN // FK, FK, FQ), F32)],
        compiler_params=pltpu.CompilerParams(vmem_limit_bytes=56 << 20),
        cost_estimate=pl.CostEstimate(flops=15 * US, bytes_accessed=3 << 20, transcendentals=8 << 20),
        name="attn_fwd",
    )(qkv)


def bwd_kernel(
    edge_ref, blk_ref, qkv_ref, se_ref, o_ref, g_ref, lse_ref, cs_ref, mod_ref, te_ref, act_ref, n_hbm, w_hbm,
    out_ref, gw_ref, kv, dq, delta, norm, wcol, sem,
):
    total = qkv_ref.shape[0] * LN
    half = blk_ref[0] // 2
    copies = [pltpu.make_async_copy(n_hbm, norm, sem.at[0])]
    for w in range(3):
        cols = pl.ds(pl.multiple_of(w * 1024 + half * LN, LN), LN)
        copies.append(pltpu.make_async_copy(w_hbm.at[:, cols], wcol.at[w], sem.at[1 + w]))
    for copy in copies:
        copy.start()

    def at_g(r):
        return pl.ds(pl.multiple_of(r * 64, 64), 64)

    def back(x, i, n):
        c, s = lanes(cs_ref, i, n, 0), lanes(cs_ref, i, n, 1)
        a, b = x[:32], x[32:]
        return jnp.concatenate([a * c + b * s, b * c - a * s], axis=0).astype(BF)

    def put(i, n, r, w, x):
        for p in range(n // LN):
            out_ref[i * (n // LN) + p, at(r, w), :] = x[:, p * LN : (p + 1) * LN]

    def row_of(ref, r, j):
        return jnp.concatenate([ref[r, j * (BQ // LN) + i, 0:1, :] for i in range(BQ // LN)], axis=-1)

    def rows(r, _):
        def prep(i, _):
            gT = g_ref[i, at_g(r), :]
            kv[pl.ds(pl.multiple_of(i * LN, LN), LN), :] = jnp.concatenate([qkv_ref[i, at(r, 1), :], qkv_ref[i, at(r, 2), :]], axis=0).T
            d = jnp.sum(gT.astype(F32) * o_ref[i, r].astype(F32), axis=0, keepdims=True)
            delta[0, i] = jnp.broadcast_to(d, (8, LN))
            return 0

        lax.fori_loop(0, total // LN, prep, 0)

        def zero(j, _):
            dq[j] = jnp.zeros((64, BQ), F32)
            return 0

        lax.fori_loop(0, total // BQ, zero, 0)

        def kblock(i, _):
            kvi = kv[pl.ds(pl.multiple_of(i * BK, BK), BK), :]
            kT = lanes(qkv_ref, i, BK, at(r, 1))
            z = jnp.zeros((64, BQ), BF)

            def make(masked):
                def body(j, c):
                    dk, dv = c
                    qT, gT = lanes(qkv_ref, j, BQ, at(r, 0)), lanes(g_ref, j, BQ, at_g(r))
                    s = dot(kvi, jnp.concatenate([qT, z], axis=0))
                    p = jnp.exp(s - row_of(lse_ref, r, j))
                    if masked:
                        start, end = spans(se_ref, r, j, BQ)
                        p = jnp.where(in_range(i, BK, start, end), p, 0.0)
                    dp = dot(kvi, jnp.concatenate([z, gT], axis=0))
                    ds = (p * (dp - row_of(delta, 0, j))).astype(BF)
                    dv = dv + nt(gT, p.astype(BF))
                    dk = dk + nt(qT, ds)
                    dq[j] = dq[j] + dot(kT, ds)
                    return dk, dv

                return body

            zz = jnp.zeros((64, BK), F32)
            (dk, dv), _, _ = over_blocks(edge_ref, r, i, BK, BQ, make, (zz, zz))
            put(i, BK, r, 1, back(dk, i, BK))
            put(i, BK, r, 2, dv.astype(BF))
            return 0

        lax.fori_loop(0, total // BK, kblock, 0)

        def fin(j, _):
            put(j, BQ, r, 0, back(dq[j] * 0.125, j, BQ))
            return 0

        lax.fori_loop(0, total // BQ, fin, 0)
        return 0

    lax.fori_loop(0, 2, rows, 0)
    for copy in copies:
        copy.wait()
    even = blk_ref[0] % 2 == 0
    ws = []
    for i in range(3):
        t = wcol[i].astype(F32).T
        ws.append(jnp.where(even, t[:64], t[64:]))
    w = jnp.concatenate(ws, axis=0)
    ns = total // LN
    width = w.shape[1]
    grad = jnp.zeros_like(w)
    bias = jnp.zeros((192, 1), F32)
    parts = []
    for r in range(2):
        gt = jnp.concatenate([out_ref[s, r * 192 : (r + 1) * 192, :] for s in range(ns)], axis=-1)
        m = dot(gt, norm[:, r * LN : (r + 1) * LN, :].reshape(total, width))
        sv = jnp.sum(gt.astype(F32), axis=1, keepdims=True)
        bias += sv
        grad += m * (1.0 + mod_ref[r : r + 1, width:]) + sv * mod_ref[r : r + 1, :width]
        parts.append(
            jnp.concatenate([jnp.sum(w * sv, axis=0, keepdims=True), jnp.sum(w * m, axis=0, keepdims=True)], axis=-1)
        )
    gw_ref[:, :192] = grad.T.astype(BF)
    lane = lax.broadcasted_iota(jnp.int32, (8, 64), 1)
    column = jnp.zeros((8, 64), F32)
    for i in range(24):
        column = jnp.where(lane == 2 + i, bias[8 * i : 8 * i + 8], column)
    extra = act_ref[...].astype(F32).reshape(width // 8, 8, 64) + column[None]
    gw_ref[:, 192:256] = extra.reshape(width, 64).astype(BF)
    for k in range(ns):
        mine = [v[:, k * LN : (k + 1) * LN] for v in parts] + [jnp.zeros((14, LN), F32)]
        out_ref[k, SEG : SEG + 16, :] = jnp.concatenate(mine, axis=0).astype(BF)
        out_ref[k, SEG + 16 :, :] = te_ref[...]


def attn_bwd(edges, blk, qkv, se, o, g, lse, cs, mod1, time_early, act, norm, w_qkv):
    ns = qkv.shape[0]
    width = w_qkv.shape[0]
    vm = pl.BlockSpec(memory_space=pltpu.VMEM)
    sm = pl.BlockSpec(memory_space=pltpu.SMEM)
    hbm = pl.BlockSpec(memory_space=pl.ANY)
    V = pltpu.VMEM
    return pl.pallas_call(
        bwd_kernel,
        in_specs=[sm] * 2 + [vm] * 9 + [hbm] * 2,
        out_specs=[vm, vm],
        out_shape=[jax.ShapeDtypeStruct((ns, GROWS, LN), BF), jax.ShapeDtypeStruct((width, 384), BF)],
        scratch_shapes=[
            V((ns * LN, LN), BF), V((ns * LN // BQ, 64, BQ), F32), V((1, ns, 8, LN), F32),
            V(norm.shape, BF), V((3, width, LN), BF), pltpu.SemaphoreType.DMA((4,)),
        ],
        compiler_params=pltpu.CompilerParams(vmem_limit_bytes=56 << 20),
        cost_estimate=pl.CostEstimate(flops=34 * US, bytes_accessed=15 << 20, transcendentals=8 << 20),
        name="attn_bwd",
    )(edges, blk, qkv, se, o, g, lse, cs, mod1, time_early, act, norm, w_qkv)

HEADS = 16
HD = 64
D = 1024
FF = 2048
NB = 8
NK = 16
EPS = 1e-06
FR = 128
FC = 512
RT = 32


def nt(a, b):
    return lax.dot_general(a, b, (((1,), (1,)), ((), ())), preferred_element_type=F32)


def normed(x):
    center = x - jnp.mean(x, axis=-1, keepdims=True)
    inv = lax.rsqrt(jnp.mean(center * center, axis=-1, keepdims=True) + EPS)
    return center * inv, inv


def fold(x):
    return jnp.sum(x.reshape(x.shape[0] // 8, 8, x.shape[1]), axis=0)


def row_tiles(body):
    for r in range(2):

        def step(t, _, r=r):
            body(r, pl.ds(pl.multiple_of(r * FR + t * RT, RT), RT))
            return 0

        lax.fori_loop(0, FR // RT, step, 0)


def pre_kernel(
    x_ref, t_ref, bm_ref, bq_ref, cs_ref, seg_ref, wm_hbm, wq_hbm, send_ref, n1_ref, mod_ref, wm, wq, nf, h1, sem
):
    first = pltpu.make_async_copy(wm_hbm.at[:, pl.ds(0, 2 * D)], wm, sem.at[0])
    first.start()
    copies = [
        pltpu.make_async_copy(wq_hbm.at[:, pl.ds(i * 256, 256)], wq.at[i], sem.at[1 + i]) for i in range(12)
    ]
    for g in range(4):
        for w in range(3):
            copies[4 * w + g].start()

    def normalize(r, rows):
        n, _ = normed(x_ref[rows, :].astype(F32))
        n1_ref[rows, :] = n.astype(BF)
        nf[rows, :] = n

    row_tiles(normalize)
    t = t_ref[...].astype(F32)
    act = (t / (1.0 + jnp.exp(-t))).astype(BF)
    bm, bq = bm_ref[:16, :].astype(F32), bq_ref[...].astype(F32)
    first.wait()
    mod_ref[...] = dot(act, wm[...]) + jnp.concatenate([bm[i : i + 1] for i in range(16)], axis=-1)

    def modulate(r, rows):
        h1[rows, :] = (nf[rows, :] * (1.0 + mod_ref[r : r + 1, D:]) + mod_ref[r : r + 1, :D]).astype(BF)

    row_tiles(modulate)
    c = jnp.concatenate([cs_ref[0], cs_ref[0]], axis=-1)
    s = jnp.concatenate([cs_ref[1], cs_ref[1]], axis=-1)
    tile = jnp.concatenate([seg_ref[...].astype(F32), jnp.zeros((14, FR), F32)], axis=0).astype(BF)
    for g in range(4):
        for w in range(3):
            i = 4 * w + g
            copies[i].wait()
            p = (dot(h1[...], wq[i]) + jnp.concatenate([bq[2 * i : 2 * i + 1], bq[2 * i + 1 : 2 * i + 2]], axis=-1)).T
            for h in range(4):
                y = p[h * HD : (h + 1) * HD]
                if w < 2:
                    a, b = y[:32], y[32:]
                    y = jnp.concatenate([a * c - b * s, b * c + a * s], axis=0)
                    if w == 0:
                        y = y * 0.125
                y = y.astype(BF)
                send_ref[4 * g + h, w * HD : (w + 1) * HD, :] = y[:, :FR]
                send_ref[4 * g + h, (3 + w) * HD : (4 + w) * HD, :] = y[:, FR:]
        for h in range(4):
            send_ref[4 * g + h, SEG:, :] = tile


def pre(x, t, b_mod, b_qkv, cs_me, segments, w_mod, w_qkv):
    vm = pl.BlockSpec(memory_space=pltpu.VMEM)
    hbm = pl.BlockSpec(memory_space=pl.ANY)
    S = jax.ShapeDtypeStruct
    V = pltpu.VMEM
    return pl.pallas_call(
        pre_kernel,
        in_specs=[vm] * 6 + [hbm] * 2,
        out_specs=[vm] * 3,
        out_shape=[S((HEADS, SEG + 16, FR), BF), S((256, D), BF), S((2, 2 * D), F32)],
        scratch_shapes=[V((D, 2 * D), BF), V((12, D, 256), BF), V((256, D), F32), V((256, D), BF), pltpu.SemaphoreType.DMA((13,))],
        compiler_params=pltpu.CompilerParams(vmem_limit_bytes=60 << 20),
        cost_estimate=pl.CostEstimate(flops=8 * US, bytes_accessed=13 << 20, transcendentals=0),
        name="pre",
    )(x, t, b_mod, b_qkv, cs_me, segments, w_mod, w_qkv)


def mid_kernel(
    core_ref, oT_ref, x_ref, cot_ref, mod_ref, bo_ref, bu_ref, bd_ref, wo_hbm, wu_hbm, wd_hbm,
    out_ref, gm_ref, go_ref, a_ref, keep_ref, send_ref,
    wo, wu, wd, b1, mdl, n2, iv, b2, gh2, gb, sums, bsum, sem,
):
    copies = [pltpu.make_async_copy(wo_hbm, wo, sem.at[0])]
    for f in range(4):
        copies.append(pltpu.make_async_copy(wu_hbm.at[:, pl.ds(f * FC, FC)], wu.at[f], sem.at[1 + f]))
        copies.append(pltpu.make_async_copy(wd_hbm.at[pl.ds(f * FC, FC), :], wd.at[f], sem.at[5 + f]))
    for copy in copies:
        copy.start()
    low = core_ref[0] == 0

    def divide(rows, at, g):
        w = g.shape[1] // 2
        a, b = g[:, :w], g[:, w:]
        keep_ref[rows, at : at + w] = jnp.where(low, a, b)
        send_ref[rows, at : at + w] = jnp.where(low, b, a)

    sums[...] = jnp.zeros_like(sums)
    bsum[...] = jnp.zeros_like(bsum)
    o = jnp.concatenate([oT_ref[:, r].reshape(D, FR).T for r in range(2)], axis=0)
    a_ref[:, :D] = o
    copies[0].wait()
    b1[...] = dot(o, wo[...])

    def first(r, rows):
        gate1, shift2 = mod_ref[r : r + 1, :D], mod_ref[r : r + 1, D : 2 * D]
        scale2, gate2 = mod_ref[r : r + 1, 2 * D : 3 * D], mod_ref[r : r + 1, 3 * D :]
        branch = b1[rows, :] + bo_ref[...].astype(F32)
        b1[rows, :] = branch
        middle = x_ref[rows, :].astype(F32) + gate1 * branch
        mdl[rows, :] = middle
        n, inv = normed(middle)
        n2[rows, :] = n
        iv[rows, :] = jnp.broadcast_to(inv, (RT, FR))
        a_ref[rows, D : 2 * D] = (n * (1.0 + scale2) + shift2).astype(BF)
        g = (gate2 * cot_ref[rows, :].astype(F32)).astype(BF)
        gb[rows, :] = g
        divide(rows, 3 * FC, g)
        bsum[:, 3 * D :] += fold(g.astype(F32))

    row_tiles(first)
    for f in range(4):
        copies[1 + 2 * f].wait()
        copies[2 + 2 * f].wait()
        u = dot(a_ref[:, D : 2 * D], wu[f]) + bu_ref[:, f * FC : (f + 1) * FC].astype(F32)
        k = math.sqrt(2.0 / math.pi)
        sq = u * u
        t = jnp.tanh(u * (k + (k * 0.044715) * sq))
        half = 0.5 * (1.0 + t)
        a = (u * half).astype(BF)
        a_ref[:, 2 * D + f * FC : 2 * D + (f + 1) * FC] = a
        slope = half + (0.5 * u) * (1.0 - t * t) * (k + (3.0 * k * 0.044715) * sq)
        gu = (nt(gb[...], wd[f]) * slope).astype(BF)
        at = FC + (f % 2) * FC

        @pl.when(low == (f < 2))
        def _(gu=gu, at=at):
            keep_ref[:, at : at + FC] = gu

        @pl.when(low != (f < 2))
        def _(gu=gu, at=at):
            send_ref[:, at : at + FC] = gu

        bsum[:, D + f * FC : D + (f + 1) * FC] += fold(gu.astype(F32))
        if f == 0:
            b2[...] = dot(a, wd[f])
            gh2[...] = nt(gu, wu[f])
        else:
            b2[...] += dot(a, wd[f])
            gh2[...] += nt(gu, wu[f])

    def last(r, rows):
        gate1, scale2, gate2 = mod_ref[r : r + 1, :D], mod_ref[r : r + 1, 2 * D : 3 * D], mod_ref[r : r + 1, 3 * D :]
        branch = b2[rows, :] + bd_ref[...].astype(F32)
        cot = cot_ref[rows, :].astype(F32)
        out_ref[rows, :] = (mdl[rows, :] + gate2 * branch).astype(BF)
        sums[r, :, 3 * D :] += fold(branch * cot)
        gh, n = gh2[rows, :], n2[rows, :]
        sums[r, :, D : 2 * D] += fold(gh)
        sums[r, :, 2 * D : 3 * D] += fold(gh * n)
        g = gh * (1.0 + scale2)
        back = g - jnp.mean(g, axis=-1, keepdims=True) - n * jnp.mean(g * n, axis=-1, keepdims=True)
        gm = cot + iv[rows, :1] * back
        gm_ref[rows, :] = gm
        sums[r, :, :D] += fold(b1[rows, :] * gm)
        g1 = (gate1 * gm).astype(BF)
        gb[rows, :] = g1
        divide(rows, 0, g1)
        bsum[:, :D] += fold(g1.astype(F32))

    row_tiles(last)
    goT = nt(wo[...], gb[...]).astype(BF)
    part = [jnp.sum(sums[r], axis=0, keepdims=True) for r in range(2)]
    bias = jnp.sum(bsum[...], axis=0, keepdims=True)
    for k in range(NK):
        go_ref[k, 0:HD] = goT[k * HD : (k + 1) * HD, :FR]
        go_ref[k, HD : 2 * HD] = goT[k * HD : (k + 1) * HD, FR:]
        at = lambda v, i: v[:, (2 * k + i) * FR : (2 * k + i + 1) * FR]
        tile = [at(part[0], 0), at(part[0], 1), at(part[1], 0), at(part[1], 1), at(bias, 0), at(bias, 1)]
        go_ref[k, 2 * HD :] = jnp.concatenate(tile + [jnp.zeros((10, FR), F32)], axis=0).astype(BF)


def mid(core, oT, x, cot, mod2, b_out, b_up, b_down, w_out, w_up, w_down):
    vm = pl.BlockSpec(memory_space=pltpu.VMEM)
    hbm = pl.BlockSpec(memory_space=pl.ANY)
    S = jax.ShapeDtypeStruct
    V = pltpu.VMEM
    return pl.pallas_call(
        mid_kernel,
        in_specs=[pl.BlockSpec(memory_space=pltpu.SMEM)] + [vm] * 7 + [hbm] * 3,
        out_specs=[vm] * 6,
        out_shape=[
            S((256, D), BF), S((256, D), F32), S((NK, 144, FR), BF), S((256, 4 * D), BF),
            S((256, 2 * D), BF), S((256, 2 * D), BF),
        ],
        scratch_shapes=[
            V((D, D), BF), V((4, D, FC), BF), V((4, FC, D), BF), V((256, D), F32), V((256, D), F32),
            V((256, D), F32), V((256, FR), F32), V((256, D), F32), V((256, D), F32), V((256, D), BF),
            V((2, 8, 4 * D), F32), V((8, 4 * D), F32), pltpu.SemaphoreType.DMA((9,)),
        ],
        compiler_params=pltpu.CompilerParams(vmem_limit_bytes=48 << 20),
        cost_estimate=pl.CostEstimate(flops=13 * US, bytes_accessed=16 << 20, transcendentals=256 * FF),
        name="mid",
    )(core, oT, x, cot, mod2, b_out, b_up, b_down, w_out, w_up, w_down)


def dw_kernel(oa, ob, ha, hb, aa, ab, ga, gb, out_ref):
    both = lambda a, b: jnp.concatenate([a[...].T, b[...].T], axis=-1)
    frames = lambda i, j: jnp.concatenate([ga[:, i:j], gb[:, i:j]], axis=0)
    out = dot(both(oa, ob), frames(0, FC)).reshape(NK, 8, FC)
    up = dot(both(ha, hb), frames(FC, 3 * FC)).reshape(NK, 8, 2 * FC)
    down = dot(both(aa, ab), frames(3 * FC, 4 * FC)).reshape(NK, 16, FC)
    out_ref[0, :, :, :FC] = down.astype(BF)
    out_ref[0, :, :, FC : 2 * FC] = jnp.concatenate([out, up[..., :FC]], axis=1).astype(BF)
    half = FC // 2
    out_ref[0, :, :, 2 * FC :] = jnp.concatenate([up[..., FC : FC + half], up[..., FC + half :]], axis=1).astype(BF)


def dw(a, a2, g, g2):
    cols = lambda n, first: pl.BlockSpec((256, n), lambda b: (0, first + b))
    whole = pl.BlockSpec((256, 2 * D), lambda b: (0, 0))
    return pl.pallas_call(
        dw_kernel,
        grid=(NB,),
        in_specs=[cols(128, 0)] * 2 + [cols(128, 8)] * 2 + [cols(256, 8)] * 2 + [whole] * 2,
        out_specs=pl.BlockSpec((1, NK, 16, 1280), lambda b: ((b % 4) * 2 + b // 4, 0, 0, 0)),
        out_shape=jax.ShapeDtypeStruct((NB, NK, 16, 1280), BF),
        compiler_params=pltpu.CompilerParams(vmem_limit_bytes=60 << 20),
        cost_estimate=pl.CostEstimate(flops=6 * US, bytes_accessed=12 << 20, transcendentals=0),
        name="dw",
    )(a, a2, a, a2, a, a2, g, g2)


def tail_kernel(g_ref, w_ref, x_ref, gm_ref, mod_ref, out_ref, gh1):
    step = pl.program_id(0)
    acc = None
    for w in range(3):
        g = jnp.concatenate([g_ref[:, (3 * r + w) * HD : (3 * r + w + 1) * HD, :].reshape(D, FR) for r in range(2)], axis=-1)
        t = dot(w_ref[:, w * D : (w + 1) * D], g)
        acc = t if acc is None else acc + t
    gh1[step] = acc.T

    @pl.when(step == pl.num_programs(0) - 1)
    def _():
        def body(r, rows):
            n, inv = normed(x_ref[rows, :].astype(F32))
            g = jnp.concatenate([gh1[i, rows, :] for i in range(4)], axis=-1)
            g = g * (1.0 + mod_ref[r : r + 1, D:])
            back = g - jnp.mean(g, axis=-1, keepdims=True) - n * jnp.mean(g * n, axis=-1, keepdims=True)
            out_ref[rows, :] = gm_ref[rows, :] + inv * back

        row_tiles(body)


def tail(g_back, w_qkv, x, gm, mod1):
    whole = lambda shape: pl.BlockSpec(shape, lambda g: (0,) * len(shape))
    return pl.pallas_call(
        tail_kernel,
        grid=(4,),
        in_specs=[
            whole((HEADS, GROWS, FR)), pl.BlockSpec((256, 3 * D), lambda g: (g, 0)),
            whole((256, D)), whole((256, D)), whole((2, 2 * D)),
        ],
        out_specs=whole((256, D)),
        out_shape=jax.ShapeDtypeStruct((256, D), F32),
        scratch_shapes=[pltpu.VMEM((4, 256, 256), F32)],
        compiler_params=pltpu.CompilerParams(vmem_limit_bytes=60 << 20),
        cost_estimate=pl.CostEstimate(flops=8 * US, bytes_accessed=10 << 20, transcendentals=0),
        name="tail",
    )(g_back, w_qkv, x, gm, mod1)


def a2a(x, axis):
    return lax.all_to_all(x, axis, 0, 0, tiled=True)


def spread(x, axis):
    n = lax.axis_size(axis)
    return a2a(jnp.broadcast_to(x[None], (n,) + x.shape), axis)


def dg(a, b, ca, cb):
    return lax.dot_general(a, b, (((ca,), (cb,)), ((), ())), preferred_element_type=F32)


def to_core(x):
    return lax.ppermute(x, "blk", [(i, i ^ 1) for i in range(NK)])


def after(x, *others):
    return lax.optimization_barrier((x,) + others)[0]


def per_device(
    frames, time_embed, segments, w_mod, b_mod, w_qkv, b_qkv, w_out, b_out,
    w_up, b_up, w_down, b_down, cotangent,
):
    R = frames.shape[0]
    blk = lax.axis_index("blk")
    bat = lax.axis_index("batch")
    core = blk % 2
    me = bat * NK + blk
    x = frames.reshape(R * FR, D)
    time_vals = time_embed.astype(F32)
    time_act, silu_back = jax.vjp(jax.nn.silu, time_vals)
    time_low = time_act.astype(BF)

    def mod_part(a, b):
        return dg(time_low, w_mod[:, a * D : b * D], 1, 0) + b_mod[a * D : b * D].astype(F32)

    inverse = jnp.exp(jnp.arange(32, dtype=F32) * (-2.0 * math.log(10000.0) / HD))
    inverse = inverse[:, None]
    mine = (blk * FR + jnp.arange(FR, dtype=jnp.int32)).astype(F32)[None, :]
    cs_me = jnp.stack([jnp.cos(mine * inverse), jnp.sin(mine * inverse)])
    qkv_send, n1, mod1 = pre(x, time_embed, b_mod.reshape(48, FR), b_qkv.reshape(24, FR), cs_me, segments, w_mod, w_qkv)
    qkv = a2a(qkv_send, "blk")

    mod2 = mod_part(2, 6)
    pos = jnp.arange(NK * FR, dtype=F32).reshape(NK, 1, FR)
    angles = pos * inverse[None]
    cs = jnp.stack([jnp.cos(angles), jnp.sin(angles)], axis=1)
    w_mod_mine = lax.dynamic_slice_in_dim(w_mod, 2 * D + blk * 256, 256, 1)

    qkv, n1_gather = lax.optimization_barrier((qkv, n1))
    norm_all = lax.all_gather(n1_gather, "blk", axis=0, tiled=False)

    o_heads, lse, edges, se = attn_fwd(qkv)
    oT = a2a(o_heads, "blk")
    output, g_middle, go_send, a_all, g_keep, g_give = mid(
        core.astype(jnp.int32).reshape(1), oT, x, cotangent.reshape(R * FR, D), mod2, b_out[None], b_up[None], b_down[None], w_out, w_up, w_down
    )
    go = a2a(go_send, "blk")

    a2_all, g2_all = to_core(a_all), to_core(g_give)
    dws = dw(a_all, a2_all, g_keep, g2_all)
    dws, go, norm_all = lax.optimization_barrier((dws, go, norm_all))
    x4 = [[4 * y + i for i in range(4)] for y in range(2)]
    dws = lax.psum_scatter(dws.reshape(NB * 256, 1280), "batch", scatter_dimension=0, axis_index_groups=x4, tiled=True)

    early = jnp.sum(go[:, 128:134].astype(F32), axis=0).reshape(3, 256).astype(BF)
    time_early = dg(early[:2], w_mod_mine, 1, 1).astype(BF)

    act_low = time_low.reshape(R, NB * NK, 8).transpose(1, 2, 0).reshape(D, R)
    act_low = jnp.pad(act_low, ((0, 0), (0, 62)))
    g_qkvT, pack = attn_bwd(
        edges, blk.astype(jnp.int32).reshape(1), qkv, se, o_heads, go, lse, cs, mod1, time_early.reshape(16, FR),
        act_low, norm_all, w_qkv
    )
    dws = after(dws, g_qkvT).reshape(2, NK, 16, 1280)
    dw_got = lax.ppermute(
        lax.dynamic_index_in_dim(dws, 1 - bat // 4, 0, keepdims=False), "batch", [(i, i ^ 4) for i in range(NB)]
    )
    dw_keep = lax.dynamic_index_in_dim(dws, bat // 4, 0, keepdims=False)
    g_back = a2a(g_qkvT, "blk")
    time_early = jnp.sum(g_back[:, 400:416].astype(F32), axis=0).reshape(R, D)
    tile = jnp.concatenate([jnp.sum(g_back[:, 384:386].astype(F32), axis=0).astype(BF), early.reshape(6, FR)], axis=0)
    tile = jnp.broadcast_to(tile[None], (NB * NK, 8, FR)).reshape(D, FR)
    pack = lax.dynamic_update_slice(pack, tile, (0, 256)).reshape(NB * NK, 8, 384)
    pack, dw_got = lax.optimization_barrier((pack, dw_got))
    dws = (dw_keep.astype(F32) + dw_got.astype(F32)).astype(BF)
    got = a2a(pack, ("batch", "blk")).reshape(NB, NK, 8, 384)
    gq = jnp.sum(got[..., :192].astype(F32), axis=0).reshape(NK, 8, 3, HD)
    grad_w_qkv = gq.transpose(1, 2, 0, 3).reshape(8, 3 * D)
    vec = got[..., 256:]
    rows_tail = vec[:, :, :2].transpose(0, 2, 1, 3).reshape(NB * R, 2 * D)
    rows_early = vec[:, :, 2:6].reshape(NB, NK, R, 2, FR).transpose(0, 2, 1, 3, 4).reshape(NB * R, 4 * D)
    rows_all = jnp.concatenate([rows_tail, rows_early], axis=1)
    act_mine = got[:, 0, :, 192:194].transpose(0, 2, 1).reshape(NB * R, 8)
    grad_w_mod = dg(act_mine, rows_all, 0, 0)
    b_mod_sum = jnp.sum(rows_all.astype(F32), axis=0)
    grad_b_mod = lax.dynamic_slice_in_dim(b_mod_sum, me * 48, 48)
    biases = jnp.sum(vec[:, :, 6:].astype(F32), axis=0).reshape(4 * D)
    grad_b_out = lax.dynamic_slice_in_dim(biases, me * 8, 8)
    grad_b_up = lax.dynamic_slice_in_dim(biases, D + me * 16, 16)
    grad_b_down = lax.dynamic_slice_in_dim(biases, 3 * D + me * 8, 8)
    b_qkv_sum = jnp.sum(got[..., 194:218].astype(F32), axis=0).transpose(0, 2, 1).reshape(NK, 3, HD)
    b_qkv_sum = b_qkv_sum.transpose(1, 0, 2).reshape(3 * D)
    grad_b_qkv = lax.dynamic_slice_in_dim(b_qkv_sum, me * 24, 24)
    rows_mine = lax.dynamic_slice_in_dim(rows_tail, bat * R, R, 0)
    (grad_time,) = silu_back(time_early + dg(rows_mine, w_mod[:, : 2 * D], 1, 1))

    dws = a2a(after(dws, got), "blk").reshape(NK // 2, 2, 16, 1280)
    dws = jnp.sum(dws.astype(F32), axis=0)
    grad_w_down = jnp.concatenate([dws[0, :, :FC], dws[1, :, :FC]], axis=1)
    grad_w_out = jnp.concatenate([dws[0, :8, FC : 2 * FC], dws[1, :8, FC : 2 * FC]], axis=1)
    grad_w_up = jnp.concatenate(
        [v for c in range(2) for v in (dws[c, 8:, FC : 2 * FC], dws[c, :8, 2 * FC :], dws[c, 8:, 2 * FC :])], axis=1
    )

    grad_frames = tail(g_back, w_qkv, x, g_middle, mod1)
    return (
        output.reshape(R, FR, D), grad_frames.reshape(R, FR, D), grad_time, grad_w_mod, grad_b_mod, grad_w_qkv,
        grad_b_qkv, grad_w_out, grad_b_out, grad_w_up, grad_b_up, grad_w_down, grad_b_down,
    )

def solution(mesh):
    both = ("batch", "blk")
    return jax.shard_map(
        per_device,
        mesh=mesh,
        in_specs=(
            P("batch", "blk", None), P("batch", None), P("batch", "blk"),
            P(), P(), P(), P(), P(), P(), P(), P(), P(), P(),
            P("batch", "blk", None),
        ),
        out_specs=(
            P("batch", "blk", None), P("batch", "blk", None), P("batch", None),
            P(both, None), P(both), P(both, None), P(both), P(both, None), P(both),
            P(both, None), P(both), P(both, None), P(both),
        ),
        check_vma=False,
    )
```

time: 309 us -> 269 us (0.87)
  the two profiles are of different devices: /device:TPU:2 before, /device:TPU:1 now
where the time goes in v1:
time: 269 us; the launch traced here: 263 us
  Pallas kernels  91.9 us (34%)
  waiting for transfers between devices  66 us (25%)
  blocking collectives  33.7 us (13%)
  starting transfers between devices  28 us (10%)
  between operations  14.9 us (6%)
  matrix products  10.9 us (4%)
  local copies, waits for them, and re-layouts  10.6 us (4%)
  other arithmetic  7.39 us (3%)
    all_to_all x1, blocking collectives, a2a(): return lax.all_to_all(x, axis, 0, 0, tiled=True)  33.7 us
    pallas_call x1, Pallas kernels, attn_bwd(): pl.pallas_call(bwd_kernel, in_specs=[sm] * 2 + [vm] * 9 + [hbm] * 2, out_...  32.1 us
    all_to_all x5, waiting for transfers between devices, a2a(): return lax.all_to_all(x, axis, 0, 0, tiled=True)  30.5 us
    all_to_all x5, starting transfers between devices, a2a(): return lax.all_to_all(x, axis, 0, 0, tiled=True)  25.2 us
    pallas_call x1, Pallas kernels, attn_fwd(): pl.pallas_call(fwd_kernel, in_specs=[vm], out_specs=[vm, vm, pl.BlockSpec...  15.4 us
    pallas_call x1, Pallas kernels, mid(): pl.pallas_call(mid_kernel, in_specs=[pl.BlockSpec(memory_space=pltpu.SMEM...  14.2 us
    reduce_scatter x1, waiting for transfers between devices, per_device(): lax.psum_scatter(dws.reshape(NB * 256, 1280), 'batch', scatter_dimension=...  13.7 us
    pallas_call x1, Pallas kernels, pre(): pl.pallas_call(pre_kernel, in_specs=[vm] * 6 + [hbm] * 2, out_specs=[vm]...  11.3 us
  transfers between devices with their start and end apart: 10, of which 10 were waited for; matrix products, arithmetic and copies ran while one was open for 9% of the time, Pallas kernels for 31%

profile of v1, /device:TPU:1, one launch (start us, length us, event | category | flops | bytes accessed | tf_op | source)
XLA Modules:
  0.0 263.4 jit_solution(8681707021423073025)
XLA Ops:
  8.0 11.3 %pre.1 = (bf16[16,400,128]{2,1,0:T(8,128)(2,1)}, bf16[256,1024]{1,0:T(8,128)(2,1)}, f32[2,2048]{1,0:T(2,128)}) custom-call(bf16[256,1024]{1,0:T(8,128)(2,1)} %bitcast.85, bf16[2,1024]{1,0:T(2,128)(2,1)} %t_ref.1, bf16[48,128]{1,0:T(8,128)(2,1)} %bitcast.110, bf16[24,128]{1,0:T(8,128)(2,1)} %bitcast.112, f32[2,32,128]{2,1,0:T(8,128)} %pad_maximum_fusion.2.cs_ref, ...), custom_call_target="tpu_custom_call" | custom-call | flops 9200000000 | bytes 13631488 | tf_op jit(solution)/shard_map/pre/pallas_call | solution.py:394
  19.4 33.7 %all_to_all.30.qkv_ref = bf16[16,400,128]{2,1,0:T(8,128)(2,1)} all-to-all(bf16[16,400,128]{2,1,0:T(8,128)(2,1)} %get-tuple-element.37), channel_id=1, replica_groups=mesh['batch'=8,'blk'=16] {'blk'}, dimensions={0} | all-to-all | bytes 3276800 | tf_op jit(solution)/shard_map/all_to_all | solution.py:601
  53.3 15.4 %attn_fwd.1 = (bf16[16,2,64,128]{3,2,1,0:T(8,128)(2,1)}, f32[2,16,8,128]{3,2,1,0:T(8,128)}, s32[2,8]{1,0:T(2,128)}, s32[2,16,8,128]{3,2,1,0:T(8,128)}) custom-call(bf16[16,400,128]{2,1,0:T(8,128)(2,1)} %all_to_all.30.qkv_ref), custom_call_target="tpu_custom_call" | custom-call | flops 17250000896 | bytes 3145728 | tf_op jit(solution)/shard_map/attn_fwd/pallas_call | solution.py:152
  68.7 4.1 %all-to-all-start.1 = ((bf16[16,2,64,128]{3,2,1,0:T(8,128)(2,1)}), bf16[16,2,64,128]{3,2,1,0:T(8,128)(2,1)S(1)}, u32[]{:S(2)}, u32[]{:S(2)}) async-start(bf16[16,2,64,128]{3,2,1,0:T(8,128)(2,1)} %get-tuple-element.40.o_ref), calls=%async_computation.1 | async-start | bytes 1048576 | tf_op jit(solution)/shard_map/all_to_all | solution.py:601
  72.8 4.7 %fusion.2.mod_ref = f32[2,4096]{1,0:T(2,128)S(1)} fusion(bf16[1024,6144]{1,0:T(8,128)(2,1)} %wm_hbm.1, f32[4096]{0:T(1024)S(1)} %slice_convert_fusion, bf16[2,1024]{1,0:T(2,128)(2,1)S(1)} %copy-done.6), kind=kOutput, calls=%fused_computation.2 | convolution fusion | flops 16797696 | bytes 8441856 | tf_op jit(solution)/shard_map/dot_general | solution.py:610
  77.5 6.5 %all-to-all-done.1.oT_ref = bf16[16,2,64,128]{3,2,1,0:T(8,128)(2,1)S(1)} async-done(((bf16[16,2,64,128]{3,2,1,0:T(8,128)(2,1)}), bf16[16,2,64,128]{3,2,1,0:T(8,128)(2,1)S(1)}, u32[]{:S(2)}, u32[]{:S(2)}) %all-to-all-start.1) | async-done | bytes 524320 | tf_op jit(solution)/shard_map/all_to_all | solution.py:601
  84.1 14.2 %mid.1 = (bf16[256,1024]{1,0:T(8,128)(2,1)}, f32[256,1024]{1,0:T(8,128)S(1)}, bf16[16,144,128]{2,1,0:T(8,128)(2,1)}, bf16[256,4096]{1,0:T(8,128)(2,1)}, bf16[256...) custom-call(s32[1]{0:T(128)} %bitcast.core_ref, bf16[16,2,64,128]{3,2,1,0:T(8,128)(2,1)S(1)} %all-to-all-done.1.oT_ref, ...), custom_call_target="tpu_custom_call" | custom-call | flops 14949999616 | bytes 16777216 | tf_op jit(solution)/shard_map/mid/pallas_call | solution.py:515
  101.4 3.9 %all-to-all-start.2 = ((bf16[16,144,128]{2,1,0:T(8,128)(2,1)}), bf16[16,144,128]{2,1,0:T(8,128)(2,1)S(1)}, u32[]{:S(2)}, u32[]{:S(2)}) async-start(bf16[16,144,128]{2,1,0:T(8,128)(2,1)} %get-tuple-element.47), calls=%async_computation.2 | async-start | bytes 1179648 | tf_op jit(solution)/shard_map/all_to_all | solution.py:601
  107.0 9.7 %dw.1 = bf16[8,16,16,1280]{3,2,1,0:T(8,128)(2,1)} custom-call(bf16[256,4096]{1,0:T(8,128)(2,1)} %get-tuple-element.44.oa.ha.aa, bf16[256,4096]{1,0:T(8,128)(2,1)} %collective-permute-done.ob.hb.ab, bf16[256,4096]{1,0:T(8,128)(2,1)} %get-tuple-element.44.oa.ha.aa, bf16[256,4096]{1,0:T(8,128)(2,1)} %collective-permute-done.ob.hb.ab, ...), custom_call_target="tpu_custom_call" | custom-call | flops 6899999744 | bytes 12582912 | tf_op jit(solution)/shard_map/dw/pallas_call | solution.py:549
  116.7 7.5 %all-to-all-done.2.g_ref = bf16[16,144,128]{2,1,0:T(8,128)(2,1)S(1)} async-done(((bf16[16,144,128]{2,1,0:T(8,128)(2,1)}), bf16[16,144,128]{2,1,0:T(8,128)(2,1)S(1)}, u32[]{:S(2)}, u32[]{:S(2)}) %all-to-all-start.2) | async-done | bytes 589856 | tf_op jit(solution)/shard_map/all_to_all | solution.py:601
  124.2 10.3 %all-gather.3.cloned.1.call-done = bf16[4096,1024]{1,0:T(8,128)(2,1)} async-done(((bf16[256,1024]{1,0:T(8,128)(2,1)}), bf16[4096,1024]{1,0:T(8,128)(2,1)}) %all-gather.3.cloned.1.call-update) | async-done | bytes 8388624 | tf_op jit(solution)/shard_map/all_gather | solution.py:652
  138.2 1.3 convolution_convert_fusion
  140.1 32.1 %attn_bwd.1 = (bf16[16,416,128]{2,1,0:T(8,128)(2,1)}, bf16[1024,384]{1,0:T(8,128)(2,1)}) custom-call(s32[2,8]{1,0:T(2,128)} %get-tuple-element.42.edge_ref, s32[1]{0:T(128)} %bitcast.6.blk_ref, bf16[16,400,128]{2,1,0:T(8,128)(2,1)} %all_to_all.30.qkv_ref, s32[2,16,8,128]{3,2,1,0:T(8,128)} %get-tuple-element.43.se_ref, ...), custom_call_target="tpu_custom_call" | custom-call | flops 39099998208 | bytes 15728640 | tf_op jit(solution)/shard_map/attn_bwd/pallas_call | solution.py:289
  172.2 3.7 %all-to-all-start.3 = ((bf16[16,416,128]{2,1,0:T(8,128)(2,1)}), bf16[16,416,128]{2,1,0:T(8,128)(2,1)S(1)}, u32[]{:S(2)}, u32[]{:S(2)}) async-start(bf16[16,416,128]{2,1,0:T(8,128)(2,1)} %get-tuple-element.53), calls=%async_computation.3 | async-start | bytes 3407872 | tf_op jit(solution)/shard_map/all_to_all | solution.py:601
  176.0 13.7 %reduce-scatter.2.cloned.1.call-done = bf16[512,1280]{1,0:T(8,128)(2,1)} async-done(((bf16[2048,1280]{1,0:T(8,128)(2,1)}), bf16[512,1280]{1,0:T(8,128)(2,1)}) %reduce-scatter.2.cloned.1.call-update) | async-done | bytes 1310736 | tf_op jit(solution)/shard_map/reduce_scatter | solution.py:665
  192.1 8.2 %all-to-all-done.3.g_ref = bf16[16,416,128]{2,1,0:T(8,128)(2,1)S(1)} async-done(((bf16[16,416,128]{2,1,0:T(8,128)(2,1)}), bf16[16,416,128]{2,1,0:T(8,128)(2,1)S(1)}, u32[]{:S(2)}, u32[]{:S(2)}) %all-to-all-start.3) | async-done | bytes 1703968 | tf_op jit(solution)/shard_map/all_to_all | solution.py:601
  201.2 10.0 %collective-permute-done.2 = bf16[16,16,1280]{2,1,0:T(8,128)(2,1)S(1)} collective-permute-done((bf16[16,16,1280]{2,1,0:T(8,128)(2,1)S(1)}, bf16[16,16,1280]{2,1,0:T(8,128)(2,1)S(1)}, u32[]{:S(2)}, u32[]{:S(2)}) %collective-permute-start.2) | collective-permute-done | bytes 655392 | tf_op jit(solution)/shard_map/ppermute | solution.py:677
  211.2 9.7 %all-to-all-start.4 = ((bf16[128,8,384]{2,1,0:T(8,128)(2,1)}), bf16[128,8,384]{2,1,0:T(8,128)(2,1)S(1)}, u32[]{:S(2)}, u32[]{:S(2)}) async-start(bf16[128,8,384]{2,1,0:T(8,128)(2,1)} %bitcast.12), calls=%async_computation.5 | async-start | bytes 1572864 | tf_op jit(solution)/shard_map/all_to_all | solution.py:601
  221.0 9.1 %tail.1 = f32[256,1024]{1,0:T(8,128)} custom-call(bf16[16,416,128]{2,1,0:T(8,128)(2,1)} %copy-done.4, bf16[1024,3072]{1,0:T(8,128)(2,1)} %w_ref.1, bf16[256,1024]{1,0:T(8,128)(2,1)} %bitcast.86, f32[256,1024]{1,0:T(8,128)} %copy-done.3, f32[2,2048]{1,0:T(2,128)} %get-tuple-element.51.mod_ref), custom_call_target="tpu_custom_call" | custom-call | flops 9200000000 | bytes 10485760 | tf_op jit(solution)/shard_map/tail/pallas_call | solution.py:584
  231.0 2.1 fusion.7
  233.1 4.4 %all-to-all-done.4 = bf16[128,8,384]{2,1,0:T(8,128)(2,1)S(1)} async-done(((bf16[128,8,384]{2,1,0:T(8,128)(2,1)}), bf16[128,8,384]{2,1,0:T(8,128)(2,1)S(1)}, u32[]{:S(2)}, u32[]{:S(2)}) %all-to-all-start.4) | async-done | bytes 786464 | tf_op jit(solution)/shard_map/all_to_all | solution.py:601
  238.0 3.8 %all-to-all-start.5 = ((bf16[16,16,1280]{2,1,0:T(8,128)(2,1)}), bf16[16,16,1280]{2,1,0:T(8,128)(2,1)S(1)}, u32[]{:S(2)}, u32[]{:S(2)}) async-start(bf16[16,16,1280]{2,1,0:T(8,128)(2,1)} %fusion.7), calls=%async_computation.6 | async-start | bytes 1310720 | tf_op jit(solution)/shard_map/all_to_all | solution.py:601
  246.9 4.0 %fusion.17 = f32[2,1024]{1,0:T(2,128)} fusion(bf16[2,1024]{1,0:T(2,128)(2,1)S(1)} %copy-done.6, f32[2,1024]{1,0:T(2,128)S(1)} %reshape.266, bf16[1024,6144]{1,0:T(8,128)(2,1)} %wm_hbm.1, bf16[16,2048]{1,0:T(8,128)(2,1)S(1)} %bitcast.106, s32[]{:T(128)S(6)} %select_n.44), kind=kOutput, calls=%fused_computation.53 | convolution fusion | flops 8411136 | bytes 4222980 | tf_op jit(solution)/shard_map/dot_general | solution.py:610
  250.9 3.7 %all-to-all-done.5 = bf16[16,16,1280]{2,1,0:T(8,128)(2,1)S(1)} async-done(((bf16[16,16,1280]{2,1,0:T(8,128)(2,1)}), bf16[16,16,1280]{2,1,0:T(8,128)(2,1)S(1)}, u32[]{:S(2)}, u32[]{:S(2)}) %all-to-all-start.5) | async-done | bytes 655392 | tf_op jit(solution)/shard_map/all_to_all | solution.py:601
  (95 shorter events, 21.0 us)
Async XLA Ops:
  7.2 127.4 %all-gather.3.cloned.1.call-start = ((), (), s32[]{:S(2)}) async-start(), calls=%async_computation.8 | async-start | bytes 8912896 | tf_op jit(solution)/shard_map/all_gather | solution.py:652
  8.0 45.1 %copy-start.8 = (bf16[2048]{0:T(1024)(128)(2,1)S(1)}, bf16[2048]{0:T(1024)(128)(2,1)}, u32[]{:S(2)}) copy-start(bf16[2048]{0:T(1024)(128)(2,1)} %param.24) | copy-start | bytes 12292
  8.0 45.1 %copy-start.10 = (bf16[1024]{0:T(1024)(128)(2,1)S(1)}, bf16[1024]{0:T(1024)(128)(2,1)}, u32[]{:S(2)}) copy-start(bf16[1024]{0:T(1024)(128)(2,1)} %param.26) | copy-start | bytes 6148
  8.0 45.2 %copy-start.11 = (bf16[1024]{0:T(1024)(128)(2,1)S(1)}, bf16[1024]{0:T(1024)(128)(2,1)}, u32[]{:S(2)}) copy-start(bf16[1024]{0:T(1024)(128)(2,1)} %param.22) | copy-start | bytes 6148
  8.0 45.2 %copy-start.7 = (bf16[6144]{0:T(1024)(128)(2,1)S(1)}, bf16[6144]{0:T(1024)(128)(2,1)}, u32[]{:S(2)}) copy-start(bf16[6144]{0:T(1024)(128)(2,1)} %param.18) | copy-start | bytes 36868
  53.2 19.6 %copy-start.6 = (bf16[2,1024]{1,0:T(2,128)(2,1)S(1)}, bf16[2,1024]{1,0:T(2,128)(2,1)}, u32[]{:S(2)}) copy-start(bf16[2,1024]{1,0:T(2,128)(2,1)} %t_ref.1) | copy-start | bytes 12292
  68.7 15.4 %all-to-all-start.1 = ((bf16[16,2,64,128]{3,2,1,0:T(8,128)(2,1)}), bf16[16,2,64,128]{3,2,1,0:T(8,128)(2,1)S(1)}, u32[]{:S(2)}, u32[]{:S(2)}) async-start(bf16[16,2,64,128]{3,2,1,0:T(8,128)(2,1)} %get-tuple-element.40.o_ref), calls=%async_computation.1 | async-start | bytes 1048576 | tf_op jit(solution)/shard_map/all_to_all | solution.py:601
  72.8 11.3 %copy-start = (bf16[2,128,1024]{2,1,0:T(8,128)(2,1)S(1)}, bf16[2,128,1024]{2,1,0:T(8,128)(2,1)}, u32[]{:S(2)}) copy-start(bf16[2,128,1024]{2,1,0:T(8,128)(2,1)} %param.27) | copy-start | bytes 1572868
  72.8 11.3 %copy-start.1 = (bf16[2,128,1024]{2,1,0:T(8,128)(2,1)S(1)}, bf16[2,128,1024]{2,1,0:T(8,128)(2,1)}, u32[]{:S(2)}) copy-start(bf16[2,128,1024]{2,1,0:T(8,128)(2,1)} %param.14) | copy-start | bytes 1572868
  98.3 1.0 copy-start.2
  99.3 1.0 copy-start.3
  100.2 6.8 %collective-permute-start = (bf16[256,4096]{1,0:T(8,128)(2,1)}, bf16[256,4096]{1,0:T(8,128)(2,1)}, u32[]{:S(2)}, u32[]{:S(2)}) collective-permute-start(bf16[256,4096]{1,0:T(8,128)(2,1)} %get-tuple-element.44.oa.ha.aa), channel_id=1, source_target_pairs={{0,1},{1,0},{2,3},{3,2},{4,5},{5,4},{6,7},{7,6},{8,9},{9,8},{10,11... | collective-permute-start | bytes 6291464 | tf_op jit(solution)/shard_map/ppermute | solution.py:614
  101.4 5.3 %collective-permute-start.1 = (bf16[256,2048]{1,0:T(8,128)(2,1)S(1)}, bf16[256,2048]{1,0:T(8,128)(2,1)}, u32[]{:S(2)}, u32[]{:S(2)}) collective-permute-start(bf16[256,2048]{1,0:T(8,128)(2,1)S(1)} %get-tuple-element.46), channel_id=1, source_target_pairs={{0,1},{1,0},{2,3},{3,2},{4,5},{5,4},{6,7},{7,6},{8,9},{9,8},{10,11... | collective-permute-start | bytes 3145736 | tf_op jit(solution)/shard_map/ppermute | solution.py:614
  101.4 22.8 %all-to-all-start.2 = ((bf16[16,144,128]{2,1,0:T(8,128)(2,1)}), bf16[16,144,128]{2,1,0:T(8,128)(2,1)S(1)}, u32[]{:S(2)}, u32[]{:S(2)}) async-start(bf16[16,144,128]{2,1,0:T(8,128)(2,1)} %get-tuple-element.47), calls=%async_computation.2 | async-start | bytes 1179648 | tf_op jit(solution)/shard_map/all_to_all | solution.py:601
  105.3 84.4 %reduce-scatter.2.cloned.1.call-start = ((), (), s32[]{:S(2)}) async-start(), calls=%async_computation.7 | async-start | bytes 6553600 | tf_op jit(solution)/shard_map/reduce_scatter | solution.py:665
  124.2 15.9 %copy-start.5 = (bf16[16,144,128]{2,1,0:T(8,128)(2,1)}, bf16[16,144,128]{2,1,0:T(8,128)(2,1)S(1)}, u32[]{:S(2)}) copy-start(bf16[16,144,128]{2,1,0:T(8,128)(2,1)S(1)} %all-to-all-done.2.g_ref) | copy-start | bytes 1769476
  172.2 28.1 %all-to-all-start.3 = ((bf16[16,416,128]{2,1,0:T(8,128)(2,1)}), bf16[16,416,128]{2,1,0:T(8,128)(2,1)S(1)}, u32[]{:S(2)}, u32[]{:S(2)}) async-start(bf16[16,416,128]{2,1,0:T(8,128)(2,1)} %get-tuple-element.53), calls=%async_computation.3 | async-start | bytes 3407872 | tf_op jit(solution)/shard_map/all_to_all | solution.py:601
  190.8 20.4 %collective-permute-start.2 = (bf16[16,16,1280]{2,1,0:T(8,128)(2,1)S(1)}, bf16[16,16,1280]{2,1,0:T(8,128)(2,1)S(1)}, u32[]{:S(2)}, u32[]{:S(2)}) collective-permute-start(bf16[16,16,1280]{2,1,0:T(8,128)(2,1)S(1)} %dynamic-slice_bitcast_fusion), channel_id=1, source_target_pairs={{0,64},{16,80},{32,96},{48,112},{64,0},{80,16},{96,32},{112,48},{1... | collective-permute-start | bytes 1966088 | tf_op jit(solution)/shard_map/ppermute | solution.py:677
  200.3 20.6 %copy-start.4 = (bf16[16,416,128]{2,1,0:T(8,128)(2,1)}, bf16[16,416,128]{2,1,0:T(8,128)(2,1)S(1)}, u32[]{:S(2)}) copy-start(bf16[16,416,128]{2,1,0:T(8,128)(2,1)S(1)} %all-to-all-done.3.g_ref) | copy-start | bytes 5111812
  211.2 26.3 %all-to-all-start.4 = ((bf16[128,8,384]{2,1,0:T(8,128)(2,1)}), bf16[128,8,384]{2,1,0:T(8,128)(2,1)S(1)}, u32[]{:S(2)}, u32[]{:S(2)}) async-start(bf16[128,8,384]{2,1,0:T(8,128)(2,1)} %bitcast.12), calls=%async_computation.5 | async-start | bytes 1572864 | tf_op jit(solution)/shard_map/all_to_all | solution.py:601
  238.0 16.6 %all-to-all-start.5 = ((bf16[16,16,1280]{2,1,0:T(8,128)(2,1)}), bf16[16,16,1280]{2,1,0:T(8,128)(2,1)S(1)}, u32[]{:S(2)}, u32[]{:S(2)}) async-start(bf16[16,16,1280]{2,1,0:T(8,128)(2,1)} %fusion.7), calls=%async_computation.6 | async-start | bytes 1310720 | tf_op jit(solution)/shard_map/all_to_all | solution.py:601
  254.8 1.3 copy-start.9
Sparse Core Ops, SparseCore 0:
  53.3 81.2 all-gather.2
  137.0 52.6 reduce-scatter.1

commit v2 on v1

--- a/solution.py
+++ b/solution.py
@@ -161,18 +161,8 @@
     )(qkv)
 
 
-def bwd_kernel(
-    edge_ref, blk_ref, qkv_ref, se_ref, o_ref, g_ref, lse_ref, cs_ref, mod_ref, te_ref, act_ref, n_hbm, w_hbm,
-    out_ref, gw_ref, kv, dq, delta, norm, wcol, sem,
-):
+def bwd_kernel(edge_ref, qkv_ref, se_ref, o_ref, g_ref, lse_ref, cs_ref, out_ref, kv, dq, delta):
     total = qkv_ref.shape[0] * LN
-    half = blk_ref[0] // 2
-    copies = [pltpu.make_async_copy(n_hbm, norm, sem.at[0])]
-    for w in range(3):
-        cols = pl.ds(pl.multiple_of(w * 1024 + half * LN, LN), LN)
-        copies.append(pltpu.make_async_copy(w_hbm.at[:, cols], wcol.at[w], sem.at[1 + w]))
-    for copy in copies:
-        copy.start()
 
     def at_g(r):
         return pl.ds(pl.multiple_of(r * 64, 64), 64)
@@ -244,7 +234,66 @@
         return 0
 
     lax.fori_loop(0, 2, rows, 0)
-    for copy in copies:
+
+
+def attn_bwd(edges, qkv, se, o, g, lse, cs):
+    ns = qkv.shape[0]
+    vm = pl.BlockSpec(memory_space=pltpu.VMEM)
+    V = pltpu.VMEM
+    return pl.pallas_call(
+        bwd_kernel,
+        in_specs=[pl.BlockSpec(memory_space=pltpu.SMEM)] + [vm] * 6,
+        out_specs=vm,
+        out_shape=jax.ShapeDtypeStruct((ns, GROWS, LN), BF),
+        scratch_shapes=[V((ns * LN, LN), BF), V((ns * LN // BQ, 64, BQ), F32), V((1, ns, 8, LN), F32)],
+        compiler_params=pltpu.CompilerParams(vmem_limit_bytes=48 << 20),
+        cost_estimate=pl.CostEstimate(flops=29 * US, bytes_accessed=6 << 20, transcendentals=8 << 20),
+        name="attn_bwd",
+    )(edges, qkv, se, o, g, lse, cs)
+
+
+def wgrad_kernel(
+    blk_ref, go_ref, mod_ref, act_ref, g_in, n_hbm, w_hbm, wm_hbm, g_out, gw_ref, early_ref, gv, norm, wcol, wm, extra, sem
+):
+    ns, width = norm.shape[0], norm.shape[2]
+    total = ns * LN
+    parts = 4
+    each = ns // parts
+    half = blk_ref[0] // 2
+    bring = pltpu.make_async_copy(g_in.at[:, pl.ds(0, SEG), :], gv, sem.at[0])
+    bring.start()
+    chunks = [
+        pltpu.make_async_copy(n_hbm.at[pl.ds(c * each, each)], norm.at[pl.ds(c * each, each)], sem.at[1 + c])
+        for c in range(parts)
+    ]
+    for copy in chunks:
+        copy.start()
+    others = []
+    for i in range(3):
+        cols = pl.ds(pl.multiple_of(i * width + half * LN, LN), LN)
+        others.append(pltpu.make_async_copy(w_hbm.at[:, cols], wcol.at[i], sem.at[5 + i]))
+    cols = pl.ds(pl.multiple_of(2 * width + blk_ref[0] * 256, LN), 256)
+    others.append(pltpu.make_async_copy(wm_hbm.at[:, cols], wm, sem.at[8]))
+    for copy in others:
+        copy.start()
+    tile = go_ref[0].astype(F32)
+    for i in range(1, ns):
+        tile += go_ref[i].astype(F32)
+    early = jnp.concatenate(
+        [jnp.concatenate([tile[2 * i : 2 * i + 1], tile[2 * i + 1 : 2 * i + 2]], axis=-1) for i in range(3)]
+        + [jnp.zeros((5, 256), F32)], axis=0,
+    )
+    early_ref[...] = early
+    bring.wait()
+    gt = [jnp.concatenate([gv[s, r * 192 : (r + 1) * 192, :] for s in range(ns)], axis=-1) for r in range(2)]
+    m = [None, None]
+    for c in range(parts):
+        chunks[c].wait()
+        for r in range(2):
+            n = norm[c * each : (c + 1) * each, r * LN : (r + 1) * LN, :].reshape(each * LN, width)
+            t = dot(gt[r][:, c * each * LN : (c + 1) * each * LN], n)
+            m[r] = t if c == 0 else m[r] + t
+    for copy in others:
         copy.wait()
     even = blk_ref[0] % 2 == 0
     ws = []
@@ -252,53 +301,61 @@
         t = wcol[i].astype(F32).T
         ws.append(jnp.where(even, t[:64], t[64:]))
     w = jnp.concatenate(ws, axis=0)
-    ns = total // LN
-    width = w.shape[1]
     grad = jnp.zeros_like(w)
     bias = jnp.zeros((192, 1), F32)
-    parts = []
+    sums = []
     for r in range(2):
-        gt = jnp.concatenate([out_ref[s, r * 192 : (r + 1) * 192, :] for s in range(ns)], axis=-1)
-        m = dot(gt, norm[:, r * LN : (r + 1) * LN, :].reshape(total, width))
-        sv = jnp.sum(gt.astype(F32), axis=1, keepdims=True)
+        sv = jnp.sum(gt[r].astype(F32), axis=1, keepdims=True)
         bias += sv
-        grad += m * (1.0 + mod_ref[r : r + 1, width:]) + sv * mod_ref[r : r + 1, :width]
-        parts.append(
-            jnp.concatenate([jnp.sum(w * sv, axis=0, keepdims=True), jnp.sum(w * m, axis=0, keepdims=True)], axis=-1)
+        grad += m[r] * (1.0 + mod_ref[r : r + 1, width:]) + sv * mod_ref[r : r + 1, :width]
+        sums.append(
+            jnp.concatenate([jnp.sum(w * sv, axis=0, keepdims=True), jnp.sum(w * m[r], axis=0, keepdims=True)], axis=-1)
         )
+    time = nt(early[:2].astype(BF), wm[...])
+    times = [time[r : r + 1, i * LN : (i + 1) * LN] for r in range(2) for i in range(width // LN)]
+    times = jnp.concatenate(times, axis=0).astype(BF)
+    for k in range(ns):
+        mine = [v[:, k * LN : (k + 1) * LN] for v in sums] + [jnp.zeros((14, LN), F32)]
+        extra[k, :16, :] = jnp.concatenate(mine, axis=0).astype(BF)
+        extra[k, 16:, :] = times
+    put = pltpu.make_async_copy(extra, g_out.at[:, pl.ds(SEG, GROWS - SEG), :], sem.at[9])
+    put.start()
     gw_ref[:, :192] = grad.T.astype(BF)
     lane = lax.broadcasted_iota(jnp.int32, (8, 64), 1)
     column = jnp.zeros((8, 64), F32)
     for i in range(24):
         column = jnp.where(lane == 2 + i, bias[8 * i : 8 * i + 8], column)
-    extra = act_ref[...].astype(F32).reshape(width // 8, 8, 64) + column[None]
-    gw_ref[:, 192:256] = extra.reshape(width, 64).astype(BF)
-    for k in range(ns):
-        mine = [v[:, k * LN : (k + 1) * LN] for v in parts] + [jnp.zeros((14, LN), F32)]
-        out_ref[k, SEG : SEG + 16, :] = jnp.concatenate(mine, axis=0).astype(BF)
-        out_ref[k, SEG + 16 :, :] = te_ref[...]
-
-
-def attn_bwd(edges, blk, qkv, se, o, g, lse, cs, mod1, time_early, act, norm, w_qkv):
-    ns = qkv.shape[0]
+    full = act_ref[...].astype(F32).reshape(width // 8, 8, 64) + column[None]
+    gw_ref[:, 192:256] = full.reshape(width, 64).astype(BF)
+    put.wait()
+
+
+def wgrad(blk, go, mod1, act, g, norm, w_qkv, w_mod):
+    ns = g.shape[0]
     width = w_qkv.shape[0]
     vm = pl.BlockSpec(memory_space=pltpu.VMEM)
-    sm = pl.BlockSpec(memory_space=pltpu.SMEM)
     hbm = pl.BlockSpec(memory_space=pl.ANY)
+    whole = lambda shape: pl.BlockSpec(shape, lambda s: (0,) * len(shape))
+    S = jax.ShapeDtypeStruct
     V = pltpu.VMEM
     return pl.pallas_call(
-        bwd_kernel,
-        in_specs=[sm] * 2 + [vm] * 9 + [hbm] * 2,
-        out_specs=[vm, vm],
-        out_shape=[jax.ShapeDtypeStruct((ns, GROWS, LN), BF), jax.ShapeDtypeStruct((width, 384), BF)],
+        wgrad_kernel,
+        grid=(1,),
+        in_specs=[
+            pl.BlockSpec(memory_space=pltpu.SMEM), pl.BlockSpec((ns, 16, LN), lambda s: (0, 8, 0)),
+            whole(mod1.shape), whole(act.shape), hbm, hbm, hbm, hbm,
+        ],
+        out_specs=[hbm, whole((width, 256)), whole((8, 256))],
+        out_shape=[S(g.shape, BF), S((width, 256), BF), S((8, 256), F32)],
+        input_output_aliases={4: 0},
         scratch_shapes=[
-            V((ns * LN, LN), BF), V((ns * LN // BQ, 64, BQ), F32), V((1, ns, 8, LN), F32),
-            V(norm.shape, BF), V((3, width, LN), BF), pltpu.SemaphoreType.DMA((4,)),
+            V((ns, SEG, LN), BF), V(norm.shape, BF), V((3, width, LN), BF), V((width, 256), BF),
+            V((ns, GROWS - SEG, LN), BF), pltpu.SemaphoreType.DMA((10,)),
         ],
         compiler_params=pltpu.CompilerParams(vmem_limit_bytes=56 << 20),
-        cost_estimate=pl.CostEstimate(flops=34 * US, bytes_accessed=15 << 20, transcendentals=8 << 20),
-        name="attn_bwd",
-    )(edges, blk, qkv, se, o, g, lse, cs, mod1, time_early, act, norm, w_qkv)
+        cost_estimate=pl.CostEstimate(flops=7 * US, bytes_accessed=12 << 20, transcendentals=0),
+        name="wgrad",
+    )(blk, go, mod1, act, g, norm, w_qkv, w_mod)
 
 HEADS = 16
 HD = 64
@@ -342,11 +399,11 @@
     first = pltpu.make_async_copy(wm_hbm.at[:, pl.ds(0, 2 * D)], wm, sem.at[0])
     first.start()
     copies = [
-        pltpu.make_async_copy(wq_hbm.at[:, pl.ds(i * 256, 256)], wq.at[i], sem.at[1 + i]) for i in range(12)
+        pltpu.make_async_copy(wq_hbm.at[pl.ds(i * 256, 256), :], wq.at[pl.ds(i * 256, 256), :], sem.at[1 + i])
+        for i in range(4)
     ]
-    for g in range(4):
-        for w in range(3):
-            copies[4 * w + g].start()
+    for copy in copies:
+        copy.start()
 
     def normalize(r, rows):
         n, _ = normed(x_ref[rows, :].astype(F32))
@@ -364,14 +421,15 @@
         h1[rows, :] = (nf[rows, :] * (1.0 + mod_ref[r : r + 1, D:]) + mod_ref[r : r + 1, :D]).astype(BF)
 
     row_tiles(modulate)
+    for copy in copies:
+        copy.wait()
     c = jnp.concatenate([cs_ref[0], cs_ref[0]], axis=-1)
     s = jnp.concatenate([cs_ref[1], cs_ref[1]], axis=-1)
     tile = jnp.concatenate([seg_ref[...].astype(F32), jnp.zeros((14, FR), F32)], axis=0).astype(BF)
     for g in range(4):
         for w in range(3):
             i = 4 * w + g
-            copies[i].wait()
-            p = (dot(h1[...], wq[i]) + jnp.concatenate([bq[2 * i : 2 * i + 1], bq[2 * i + 1 : 2 * i + 2]], axis=-1)).T
+            p = (dot(h1[...], wq[:, i * 256 : (i + 1) * 256]) + jnp.concatenate([bq[2 * i : 2 * i + 1], bq[2 * i + 1 : 2 * i + 2]], axis=-1)).T
             for h in range(4):
                 y = p[h * HD : (h + 1) * HD]
                 if w < 2:
@@ -396,7 +454,7 @@
         in_specs=[vm] * 6 + [hbm] * 2,
         out_specs=[vm] * 3,
         out_shape=[S((HEADS, SEG + 16, FR), BF), S((256, D), BF), S((2, 2 * D), F32)],
-        scratch_shapes=[V((D, 2 * D), BF), V((12, D, 256), BF), V((256, D), F32), V((256, D), BF), pltpu.SemaphoreType.DMA((13,))],
+        scratch_shapes=[V((D, 2 * D), BF), V((D, 3 * D), BF), V((256, D), F32), V((256, D), BF), pltpu.SemaphoreType.DMA((5,))],
         compiler_params=pltpu.CompilerParams(vmem_limit_bytes=60 << 20),
         cost_estimate=pl.CostEstimate(flops=8 * US, bytes_accessed=13 << 20, transcendentals=0),
         name="pre",
@@ -404,15 +462,16 @@
 
 
 def mid_kernel(
-    core_ref, oT_ref, x_ref, cot_ref, mod_ref, bo_ref, bu_ref, bd_ref, wo_hbm, wu_hbm, wd_hbm,
+    core_ref, oT_ref, mod_ref, bo_ref, bu_ref, bd_ref, x_hbm, cot_hbm, wo_hbm, wu_hbm, wd_hbm,
     out_ref, gm_ref, go_ref, a_ref, keep_ref, send_ref,
-    wo, wu, wd, b1, mdl, n2, iv, b2, gh2, gb, sums, bsum, sem,
+    x_ref, cot_ref, wo, wu, wd, b1, mdl, n2, iv, b2, gh2, gb, sums, bsum, sem,
 ):
     copies = [pltpu.make_async_copy(wo_hbm, wo, sem.at[0])]
     for f in range(4):
         copies.append(pltpu.make_async_copy(wu_hbm.at[:, pl.ds(f * FC, FC)], wu.at[f], sem.at[1 + f]))
         copies.append(pltpu.make_async_copy(wd_hbm.at[pl.ds(f * FC, FC), :], wd.at[f], sem.at[5 + f]))
-    for copy in copies:
+    rows_in = [pltpu.make_async_copy(x_hbm, x_ref, sem.at[9]), pltpu.make_async_copy(cot_hbm, cot_ref, sem.at[10])]
+    for copy in copies[:1] + rows_in + copies[1:]:
         copy.start()
     low = core_ref[0] == 0
 
@@ -428,6 +487,8 @@
     a_ref[:, :D] = o
     copies[0].wait()
     b1[...] = dot(o, wo[...])
+    for copy in rows_in:
+        copy.wait()
 
     def first(r, rows):
         gate1, shift2 = mod_ref[r : r + 1, :D], mod_ref[r : r + 1, D : 2 * D]
@@ -514,21 +575,21 @@
     V = pltpu.VMEM
     return pl.pallas_call(
         mid_kernel,
-        in_specs=[pl.BlockSpec(memory_space=pltpu.SMEM)] + [vm] * 7 + [hbm] * 3,
+        in_specs=[pl.BlockSpec(memory_space=pltpu.SMEM)] + [vm] * 5 + [hbm] * 5,
         out_specs=[vm] * 6,
         out_shape=[
             S((256, D), BF), S((256, D), F32), S((NK, 144, FR), BF), S((256, 4 * D), BF),
             S((256, 2 * D), BF), S((256, 2 * D), BF),
         ],
         scratch_shapes=[
-            V((D, D), BF), V((4, D, FC), BF), V((4, FC, D), BF), V((256, D), F32), V((256, D), F32),
+            V((256, D), BF), V((256, D), BF), V((D, D), BF), V((4, D, FC), BF), V((4, FC, D), BF), V((256, D), F32), V((256, D), F32),
             V((256, D), F32), V((256, FR), F32), V((256, D), F32), V((256, D), F32), V((256, D), BF),
-            V((2, 8, 4 * D), F32), V((8, 4 * D), F32), pltpu.SemaphoreType.DMA((9,)),
+            V((2, 8, 4 * D), F32), V((8, 4 * D), F32), pltpu.SemaphoreType.DMA((11,)),
         ],
         compiler_params=pltpu.CompilerParams(vmem_limit_bytes=48 << 20),
         cost_estimate=pl.CostEstimate(flops=13 * US, bytes_accessed=16 << 20, transcendentals=256 * FF),
         name="mid",
-    )(core, oT, x, cot, mod2, b_out, b_up, b_down, w_out, w_up, w_down)
+    )(core, oT, mod2, b_out, b_up, b_down, x, cot, w_out, w_up, w_down)
 
 
 def dw_kernel(oa, ob, ha, hb, aa, ab, ga, gb, out_ref):
@@ -646,9 +707,10 @@
     pos = jnp.arange(NK * FR, dtype=F32).reshape(NK, 1, FR)
     angles = pos * inverse[None]
     cs = jnp.stack([jnp.cos(angles), jnp.sin(angles)], axis=1)
-    w_mod_mine = lax.dynamic_slice_in_dim(w_mod, 2 * D + blk * 256, 256, 1)
-
-    qkv, n1_gather = lax.optimization_barrier((qkv, n1))
+
+    act_low = time_low.reshape(R, NB * NK, 8).transpose(1, 2, 0).reshape(D, R)
+    act_low = jnp.pad(act_low, ((0, 0), (0, 62)))
+    qkv, n1_gather, cs, act_low = lax.optimization_barrier((qkv, n1, cs, act_low))
     norm_all = lax.all_gather(n1_gather, "blk", axis=0, tiled=False)
 
     o_heads, lse, edges, se = attn_fwd(qkv)
@@ -660,54 +722,76 @@
 
     a2_all, g2_all = to_core(a_all), to_core(g_give)
     dws = dw(a_all, a2_all, g_keep, g2_all)
-    dws, go, norm_all = lax.optimization_barrier((dws, go, norm_all))
+    dws, go = lax.optimization_barrier((dws, go))
     x4 = [[4 * y + i for i in range(4)] for y in range(2)]
     dws = lax.psum_scatter(dws.reshape(NB * 256, 1280), "batch", scatter_dimension=0, axis_index_groups=x4, tiled=True)
 
-    early = jnp.sum(go[:, 128:134].astype(F32), axis=0).reshape(3, 256).astype(BF)
-    time_early = dg(early[:2], w_mod_mine, 1, 1).astype(BF)
-
-    act_low = time_low.reshape(R, NB * NK, 8).transpose(1, 2, 0).reshape(D, R)
-    act_low = jnp.pad(act_low, ((0, 0), (0, 62)))
-    g_qkvT, pack = attn_bwd(
-        edges, blk.astype(jnp.int32).reshape(1), qkv, se, o_heads, go, lse, cs, mod1, time_early.reshape(16, FR),
-        act_low, norm_all, w_qkv
+    g_qkvT = attn_bwd(edges, qkv, se, o_heads, go, lse, cs)
+    g_qkvT, pack, early = wgrad(
+        blk.astype(jnp.int32).reshape(1), go, mod1, act_low, g_qkvT, norm_all, w_qkv, w_mod
     )
     dws = after(dws, g_qkvT).reshape(2, NK, 16, 1280)
-    dw_got = lax.ppermute(
-        lax.dynamic_index_in_dim(dws, 1 - bat // 4, 0, keepdims=False), "batch", [(i, i ^ 4) for i in range(NB)]
-    )
+    dw_give = lax.dynamic_index_in_dim(dws, 1 - bat // 4, 0, keepdims=False)
     dw_keep = lax.dynamic_index_in_dim(dws, bat // 4, 0, keepdims=False)
     g_back = a2a(g_qkvT, "blk")
+    dw_got = lax.ppermute(dw_give, "batch", [(i, i ^ 4) for i in range(NB)])
+
+    tail_mine = jnp.sum(g_back[:, 384:386].astype(F32), axis=0).astype(BF)
     time_early = jnp.sum(g_back[:, 400:416].astype(F32), axis=0).reshape(R, D)
-    tile = jnp.concatenate([jnp.sum(g_back[:, 384:386].astype(F32), axis=0).astype(BF), early.reshape(6, FR)], axis=0)
-    tile = jnp.broadcast_to(tile[None], (NB * NK, 8, FR)).reshape(D, FR)
-    pack = lax.dynamic_update_slice(pack, tile, (0, 256)).reshape(NB * NK, 8, 384)
+    tile = jnp.concatenate([tail_mine.reshape(1, 256), early[:3].astype(BF), jnp.zeros((12, 256), BF)], axis=0)
+    pack = jnp.concatenate([pack.reshape(NB, FR, 256), jnp.broadcast_to(tile[None], (NB, 16, 256))], axis=1)
     pack, dw_got = lax.optimization_barrier((pack, dw_got))
-    dws = (dw_keep.astype(F32) + dw_got.astype(F32)).astype(BF)
-    got = a2a(pack, ("batch", "blk")).reshape(NB, NK, 8, 384)
-    gq = jnp.sum(got[..., :192].astype(F32), axis=0).reshape(NK, 8, 3, HD)
+    got = a2a(pack, "batch")
+    w_mod_tail = lax.dynamic_slice_in_dim(w_mod, blk * FR, FR, 1)
+    time_part = dg(tail_mine, w_mod_tail, 1, 1)
+    gw_rows = jnp.sum(got[:, :FR, :192].astype(F32), axis=0)
+    s_sum = jnp.sum(got[:, :8, 194:218].astype(F32), axis=0)
+    tiles = got[:, FR : FR + 4]
+    rows = jnp.concatenate([tiles[:, 0].reshape(NB * R, FR), tiles[:, 1:3].reshape(NB * R, 2 * FR)], axis=1)
+    act_rows = got[:, :FR, 192:194].transpose(0, 2, 1).reshape(NB * R, FR)
+    outer = dg(act_rows, rows, 0, 0)
+
+    def wide(v, n):
+        return jnp.broadcast_to(v.reshape(1, 8, n), (NK, 8, n))
+
+    dws = dw_keep.astype(F32) + dw_got.astype(F32)
+    pack3 = jnp.concatenate(
+        [
+            outer.reshape(NK, 8, 384),
+            wide(time_part, 256),
+            wide(jnp.sum(rows.astype(F32), axis=0), 48),
+            wide(jnp.sum(tiles[:, 3].astype(F32), axis=0), 32),
+            wide(s_sum, 24),
+            gw_rows.reshape(NK, 8, 192),
+            jnp.zeros((NK, 8, 88), F32),
+            dws[:, :8],
+            dws[:, 8:],
+        ],
+        axis=-1,
+    ).astype(BF)
+    got = a2a(pack3, "blk")
+    gq = got[:, :, 744:936].astype(F32).reshape(NK, 8, 3, HD)
     grad_w_qkv = gq.transpose(1, 2, 0, 3).reshape(8, 3 * D)
-    vec = got[..., 256:]
-    rows_tail = vec[:, :, :2].transpose(0, 2, 1, 3).reshape(NB * R, 2 * D)
-    rows_early = vec[:, :, 2:6].reshape(NB, NK, R, 2, FR).transpose(0, 2, 1, 3, 4).reshape(NB * R, 4 * D)
-    rows_all = jnp.concatenate([rows_tail, rows_early], axis=1)
-    act_mine = got[:, 0, :, 192:194].transpose(0, 2, 1).reshape(NB * R, 8)
-    grad_w_mod = dg(act_mine, rows_all, 0, 0)
-    b_mod_sum = jnp.sum(rows_all.astype(F32), axis=0)
+    grad_w_mod = jnp.concatenate(
+        [
+            got[:, :, :FR].transpose(1, 0, 2).reshape(8, 2 * D),
+            got[:, :, FR : 3 * FR].transpose(1, 0, 2).reshape(8, 4 * D),
+        ],
+        axis=1,
+    ).astype(F32)
+    (grad_time,) = silu_back(time_early + jnp.sum(got[:, :, 384:640].astype(F32), axis=0).reshape(R, D))
+    b_mod = got[:, :, 640:688].astype(F32).reshape(NK, 384)
+    b_mod_sum = jnp.concatenate([b_mod[:, :FR].reshape(-1), b_mod[:, FR:].reshape(-1)])
     grad_b_mod = lax.dynamic_slice_in_dim(b_mod_sum, me * 48, 48)
-    biases = jnp.sum(vec[:, :, 6:].astype(F32), axis=0).reshape(4 * D)
+    biases = got[:, :, 688:720].astype(F32).reshape(-1)
     grad_b_out = lax.dynamic_slice_in_dim(biases, me * 8, 8)
     grad_b_up = lax.dynamic_slice_in_dim(biases, D + me * 16, 16)
     grad_b_down = lax.dynamic_slice_in_dim(biases, 3 * D + me * 8, 8)
-    b_qkv_sum = jnp.sum(got[..., 194:218].astype(F32), axis=0).transpose(0, 2, 1).reshape(NK, 3, HD)
+    b_qkv_sum = got[:, :, 720:744].astype(F32).transpose(0, 2, 1).reshape(NK, 3, HD)
     b_qkv_sum = b_qkv_sum.transpose(1, 0, 2).reshape(3 * D)
     grad_b_qkv = lax.dynamic_slice_in_dim(b_qkv_sum, me * 24, 24)
-    rows_mine = lax.dynamic_slice_in_dim(rows_tail, bat * R, R, 0)
-    (grad_time,) = silu_back(time_early + dg(rows_mine, w_mod[:, : 2 * D], 1, 1))
-
-    dws = a2a(after(dws, got), "blk").reshape(NK // 2, 2, 16, 1280)
-    dws = jnp.sum(dws.astype(F32), axis=0)
+    dws = jnp.sum(got[:, :, 1024:].astype(F32).reshape(NK // 2, 2, 8, 2560), axis=0)
+    dws = jnp.concatenate([dws[..., :1280], dws[..., 1280:]], axis=1)
     grad_w_down = jnp.concatenate([dws[0, :, :FC], dws[1, :, :FC]], axis=1)
     grad_w_out = jnp.concatenate([dws[0, :8, FC : 2 * FC], dws[1, :8, FC : 2 * FC]], axis=1)
     grad_w_up = jnp.concatenate(

time: 269 us -> 258 us (0.959); the launches traced: 263 us -> 257 us
  blocking collectives: 33.7 us -> 0 us
  waiting for transfers between devices: 66 us -> 78.8 us
  starting transfers between devices: 28 us -> 40 us
  local copies, waits for them, and re-layouts: 10.6 us -> 16.1 us
  matrix products: 10.9 us -> 5.97 us
    all_to_all x1 -> x0, blocking collectives: 33.7 us -> none  [a2a(): return lax.all_to_all(x, axis, 0, 0, tiled=True)]
    all_to_all x5 -> x6, waiting for transfers between devices: 30.5 us -> 58.4 us  [a2a(): return lax.all_to_all(x, axis, 0, 0, tiled=True)]
    all_to_all x5 -> x6, starting transfers between devices: 25.2 us -> 37.4 us  [a2a(): return lax.all_to_all(x, axis, 0, 0, tiled=True)]
    all_gather x1, waiting for transfers between devices: 10.3 us -> 0.01 us  [per_device(): norm_all = lax.all_gather(n1_gather, 'blk', axis=0, tiled=False)]
    unnamed x31 -> x53, local copies, waits for them, and re-layouts: 2.03 us -> 7.36 us
    dot_general x4 -> x3, matrix products: 10.9 us -> 5.97 us  [dg(): lax.dot_general(a, b, (((ca,), (cb,)), ((), ())), preferred_element_type=...]
    reduce_scatter x1, waiting for transfers between devices: 13.7 us -> 10.2 us  [per_device(): lax.psum_scatter(dws.reshape(NB * 256, 1280), 'batch', scatter_dimension=...]
    pallas_call x1, Pallas kernels: 11.3 us -> 8.29 us  [pre(): pl.pallas_call(pre_kernel, in_specs=[vm] * 6 + [hbm] * 2, out_specs=[vm]...]
  transfers between devices with their start and end apart: 10 -> 11, of which waited for: 10 -> 10; matrix products, arithmetic and copies ran while one was open for 9% -> 5% of each run, Pallas kernels for 31% -> 33%
where the time goes in v2:
time: 258 us; the launch traced here: 257 us
  Pallas kernels  91.9 us (36%)
  waiting for transfers between devices  78.8 us (31%)
  starting transfers between devices  40 us (16%)
  local copies, waits for them, and re-layouts  16.1 us (6%)
  between operations  16.1 us (6%)
  other arithmetic  8.24 us (3%)
  matrix products  5.97 us (2%)
    all_to_all x6, waiting for transfers between devices, a2a(): return lax.all_to_all(x, axis, 0, 0, tiled=True)  58.4 us
    all_to_all x6, starting transfers between devices, a2a(): return lax.all_to_all(x, axis, 0, 0, tiled=True)  37.4 us
    pallas_call x1, Pallas kernels, attn_bwd(): pl.pallas_call(bwd_kernel, in_specs=[pl.BlockSpec(memory_space=pltpu.SMEM...  26.8 us
    pallas_call x1, Pallas kernels, attn_fwd(): pl.pallas_call(fwd_kernel, in_specs=[vm], out_specs=[vm, vm, pl.BlockSpec...  15.6 us
    pallas_call x1, Pallas kernels, mid(): pl.pallas_call(mid_kernel, in_specs=[pl.BlockSpec(memory_space=pltpu.SMEM...  14.2 us
    reduce_scatter x1, waiting for transfers between devices, per_device(): lax.psum_scatter(dws.reshape(NB * 256, 1280), 'batch', scatter_dimension=...  10.2 us
    pallas_call x1, Pallas kernels, dw(): pl.pallas_call(dw_kernel, grid=(NB,), in_specs=[cols(128, 0)] * 2 + [cols...  9.61 us
    pallas_call x1, Pallas kernels, tail(): pl.pallas_call(tail_kernel, grid=(4,), in_specs=[whole((HEADS, GROWS, FR)...  9.13 us
  transfers between devices with their start and end apart: 11, of which 10 were waited for; matrix products, arithmetic and copies ran while one was open for 5% of the time, Pallas kernels for 33%

profile of v2, /device:TPU:1, one launch (start us, length us, event | category | flops | bytes accessed | tf_op | source)
XLA Modules:
  0.0 257.1 jit_solution(7679198433812288319)
XLA Ops:
  8.8 8.3 %pre.1 = (bf16[16,400,128]{2,1,0:T(8,128)(2,1)}, bf16[256,1024]{1,0:T(8,128)(2,1)}, f32[2,2048]{1,0:T(2,128)}) custom-call(bf16[256,1024]{1,0:T(8,128)(2,1)} %bitcast.92, bf16[2,1024]{1,0:T(2,128)(2,1)} %t_ref.1, bf16[48,128]{1,0:T(8,128)(2,1)} %bitcast.109, bf16[24,128]{1,0:T(8,128)(2,1)} %bitcast.112, f32[2,32,128]{2,1,0:T(8,128)} %pad_maximum_fusion.4.cs_ref, ...), custom_call_target="tpu_custom_call" | custom-call | flops 9200000000 | bytes 13631488 | tf_op jit(solution)/shard_map/pre/pallas_call | solution.py:452
  17.1 9.5 %all-to-all-start = ((bf16[16,400,128]{2,1,0:T(8,128)(2,1)}), bf16[16,400,128]{2,1,0:T(8,128)(2,1)S(1)}, u32[]{:S(2)}, u32[]{:S(2)}) async-start(bf16[16,400,128]{2,1,0:T(8,128)(2,1)} %get-tuple-element.38), calls=%async_computation | async-start | bytes 3276800 | tf_op jit(solution)/shard_map/all_to_all | solution.py:662
  29.5 20.6 %all-to-all-done.qkv_ref = bf16[16,400,128]{2,1,0:T(8,128)(2,1)S(1)} async-done(((bf16[16,400,128]{2,1,0:T(8,128)(2,1)}), bf16[16,400,128]{2,1,0:T(8,128)(2,1)S(1)}, u32[]{:S(2)}, u32[]{:S(2)}) %all-to-all-start) | async-done | bytes 1638432 | tf_op jit(solution)/shard_map/all_to_all | solution.py:662
  51.3 15.6 %attn_fwd.1 = (bf16[16,2,64,128]{3,2,1,0:T(8,128)(2,1)}, f32[2,16,8,128]{3,2,1,0:T(8,128)}, s32[2,8]{1,0:T(2,128)}, s32[2,16,8,128]{3,2,1,0:T(8,128)}) custom-call(bf16[16,400,128]{2,1,0:T(8,128)(2,1)} %copy-done.2), custom_call_target="tpu_custom_call" | custom-call | flops 17250000896 | bytes 3145728 | tf_op jit(solution)/shard_map/attn_fwd/pallas_call | solution.py:152
  67.0 5.5 %all-to-all-start.1 = ((bf16[16,2,64,128]{3,2,1,0:T(8,128)(2,1)}), bf16[16,2,64,128]{3,2,1,0:T(8,128)(2,1)S(1)}, u32[]{:S(2)}, u32[]{:S(2)}) async-start(bf16[16,2,64,128]{3,2,1,0:T(8,128)(2,1)} %get-tuple-element.41.o_ref), calls=%async_computation.1 | async-start | bytes 1048576 | tf_op jit(solution)/shard_map/all_to_all | solution.py:662
  72.4 4.7 %fusion.2.mod_ref = f32[2,4096]{1,0:T(2,128)S(1)} fusion(bf16[1024,6144]{1,0:T(8,128)(2,1)} %wm_hbm.3, f32[4096]{0:T(1024)S(1)} %slice_convert_fusion.3, bf16[2,1024]{1,0:T(2,128)(2,1)S(1)} %copy-done.15), kind=kOutput, calls=%fused_computation.2 | convolution fusion | flops 16797696 | bytes 8441856 | tf_op jit(solution)/shard_map/dot_general | solution.py:671
  77.2 6.6 %all-to-all-done.1.oT_ref = bf16[16,2,64,128]{3,2,1,0:T(8,128)(2,1)S(1)} async-done(((bf16[16,2,64,128]{3,2,1,0:T(8,128)(2,1)}), bf16[16,2,64,128]{3,2,1,0:T(8,128)(2,1)S(1)}, u32[]{:S(2)}, u32[]{:S(2)}) %all-to-all-start.1) | async-done | bytes 524320 | tf_op jit(solution)/shard_map/all_to_all | solution.py:662
  83.7 14.2 %mid.1 = (bf16[256,1024]{1,0:T(8,128)(2,1)}, f32[256,1024]{1,0:T(8,128)S(1)}, bf16[16,144,128]{2,1,0:T(8,128)(2,1)}, bf16[256,4096]{1,0:T(8,128)(2,1)}, bf16[256...) custom-call(s32[1]{0:T(128)} %bitcast.core_ref, bf16[16,2,64,128]{3,2,1,0:T(8,128)(2,1)S(1)} %all-to-all-done.1.oT_ref, ...), custom_call_target="tpu_custom_call" | custom-call | flops 14949999616 | bytes 16777216 | tf_op jit(solution)/shard_map/mid/pallas_call | solution.py:576
  101.0 3.9 %all-to-all-start.2 = ((bf16[16,144,128]{2,1,0:T(8,128)(2,1)}), bf16[16,144,128]{2,1,0:T(8,128)(2,1)S(1)}, u32[]{:S(2)}, u32[]{:S(2)}) async-start(bf16[16,144,128]{2,1,0:T(8,128)(2,1)} %get-tuple-element.46), calls=%async_computation.2 | async-start | bytes 1179648 | tf_op jit(solution)/shard_map/all_to_all | solution.py:662
  104.9 1.4 collective-permute-done.1.gb
  107.3 9.6 %dw.1 = bf16[8,16,16,1280]{3,2,1,0:T(8,128)(2,1)} custom-call(bf16[256,4096]{1,0:T(8,128)(2,1)} %get-tuple-element.43.oa.ha.aa, bf16[256,4096]{1,0:T(8,128)(2,1)} %collective-permute-done.ob.hb.ab, bf16[256,4096]{1,0:T(8,128)(2,1)} %get-tuple-element.43.oa.ha.aa, bf16[256,4096]{1,0:T(8,128)(2,1)} %collective-permute-done.ob.hb.ab, ...), custom_call_target="tpu_custom_call" | custom-call | flops 6899999744 | bytes 12582912 | tf_op jit(solution)/shard_map/dw/pallas_call | solution.py:610
  116.9 5.4 %all-to-all-done.2.g_ref.go_ref = bf16[16,144,128]{2,1,0:T(8,128)(2,1)S(1)} async-done(((bf16[16,144,128]{2,1,0:T(8,128)(2,1)}), bf16[16,144,128]{2,1,0:T(8,128)(2,1)S(1)}, u32[]{:S(2)}, u32[]{:S(2)}) %all-to-all-start.2) | async-done | bytes 589856 | tf_op jit(solution)/shard_map/all_to_all | solution.py:662
  124.1 26.8 %attn_bwd.1.g_in = bf16[16,416,128]{2,1,0:T(8,128)(2,1)S(1)} custom-call(s32[2,8]{1,0:T(2,128)S(1)} %copy-done.11, bf16[16,400,128]{2,1,0:T(8,128)(2,1)S(1)} %copy-done.3, s32[2,16,8,128]{3,2,1,0:T(8,128)S(1)} %copy-done.10, bf16[16,2,64,128]{3,2,1,0:T(8,128)(2,1)S(1)} %copy-done.4, bf16[16,144,128]{2,1,0:T(8,128)(2,1)S(1)} %all-to-all-done.2.g_ref.go_ref, ...), custom_call_target="tpu_custom_call" | custom-call | flops 33350000640 | bytes 6291456 | tf_op jit(solution)/shard_map/attn_bwd/pallas_call | solution.py:243
  152.1 8.3 %wgrad.1 = (bf16[16,416,128]{2,1,0:T(8,128)(2,1)}, bf16[1024,256]{1,0:T(8,128)(2,1)}, f32[8,256]{1,0:T(8,128)}) custom-call(s32[1]{0:T(128)} %bitcast.8.blk_ref, bf16[16,144,128]{2,1,0:T(8,128)(2,1)} %copy-done.1, f32[2,2048]{1,0:T(2,128)} %get-tuple-element.48.mod_ref, bf16[1024,64]{1,0:T(8,128)(2,1)} %pad.4.act_ref, ...), custom_call_target="tpu_custom_call", output_to_operand_aliasing={{0}: (4, {})} | custom-call | flops 8049999872 | bytes 12582912 | tf_op jit(solution)/shard_map/wgrad/pallas_call | solution.py:341
  160.5 4.3 %all-to-all-start.3 = ((bf16[16,416,128]{2,1,0:T(8,128)(2,1)}), bf16[16,416,128]{2,1,0:T(8,128)(2,1)S(1)}, u32[]{:S(2)}, u32[]{:S(2)}) async-start(bf16[16,416,128]{2,1,0:T(8,128)(2,1)} %get-tuple-element.55), calls=%async_computation.3 | async-start | bytes 3407872 | tf_op jit(solution)/shard_map/all_to_all | solution.py:662
  164.7 10.2 %reduce-scatter.2.cloned.1.call-done = bf16[512,1280]{1,0:T(8,128)(2,1)} async-done(((bf16[2048,1280]{1,0:T(8,128)(2,1)}), bf16[512,1280]{1,0:T(8,128)(2,1)}) %reduce-scatter.2.cloned.1.call-update) | async-done | bytes 1310736 | tf_op jit(solution)/shard_map/reduce_scatter | solution.py:727
  178.2 10.9 %all-to-all-done.3.g_ref = bf16[16,416,128]{2,1,0:T(8,128)(2,1)S(1)} async-done(((bf16[16,416,128]{2,1,0:T(8,128)(2,1)}), bf16[16,416,128]{2,1,0:T(8,128)(2,1)S(1)}, u32[]{:S(2)}, u32[]{:S(2)}) %all-to-all-start.3) | async-done | bytes 1703968 | tf_op jit(solution)/shard_map/all_to_all | solution.py:662
  190.3 8.3 %collective-permute-done.2 = bf16[16,16,1280]{2,1,0:T(8,128)(2,1)S(1)} collective-permute-done((bf16[16,16,1280]{2,1,0:T(8,128)(2,1)S(1)}, bf16[16,16,1280]{2,1,0:T(8,128)(2,1)S(1)}, u32[]{:S(2)}, u32[]{:S(2)}) %collective-permute-start.2) | collective-permute-done | bytes 655392 | tf_op jit(solution)/shard_map/ppermute | solution.py:737
  199.4 5.3 %all-to-all-start.4 = ((bf16[8,144,256]{2,1,0:T(8,128)(2,1)}), bf16[8,144,256]{2,1,0:T(8,128)(2,1)S(1)}, u32[]{:S(2)}, u32[]{:S(2)}) async-start(bf16[8,144,256]{2,1,0:T(8,128)(2,1)} %pad_maximum_fusion), calls=%async_computation.5 | async-start | bytes 1179648 | tf_op jit(solution)/shard_map/all_to_all | solution.py:662
  205.8 1.5 fusion.5
  207.3 8.2 %all-to-all-done.4 = bf16[8,144,256]{2,1,0:T(8,128)(2,1)S(1)} async-done(((bf16[8,144,256]{2,1,0:T(8,128)(2,1)}), bf16[8,144,256]{2,1,0:T(8,128)(2,1)S(1)}, u32[]{:S(2)}, u32[]{:S(2)}) %all-to-all-start.4) | async-done | bytes 589856 | tf_op jit(solution)/shard_map/all_to_all | solution.py:662
  217.8 9.1 %all-to-all-start.5 = ((bf16[16,8,3584]{2,1,0:T(8,128)(2,1)}), bf16[16,8,3584]{2,1,0:T(8,128)(2,1)S(1)}, u32[]{:S(2)}, u32[]{:S(2)}) async-start(bf16[16,8,3584]{2,1,0:T(8,128)(2,1)} %concatenate.34), calls=%async_computation.6 | async-start | bytes 1835008 | tf_op jit(solution)/shard_map/all_to_all | solution.py:662
  226.9 9.1 %tail.1 = f32[256,1024]{1,0:T(8,128)} custom-call(bf16[16,416,128]{2,1,0:T(8,128)(2,1)} %copy-done.12, bf16[1024,3072]{1,0:T(8,128)(2,1)} %w_ref.1, bf16[256,1024]{1,0:T(8,128)(2,1)} %bitcast.93, f32[256,1024]{1,0:T(8,128)} %copy-done.8, f32[2,2048]{1,0:T(2,128)} %get-tuple-element.48.mod_ref), custom_call_target="tpu_custom_call" | custom-call | flops 9200000000 | bytes 10485760 | tf_op jit(solution)/shard_map/tail/pallas_call | solution.py:645
  236.0 6.7 %all-to-all-done.5 = bf16[16,8,3584]{2,1,0:T(8,128)(2,1)S(1)} async-done(((bf16[16,8,3584]{2,1,0:T(8,128)(2,1)}), bf16[16,8,3584]{2,1,0:T(8,128)(2,1)S(1)}, u32[]{:S(2)}, u32[]{:S(2)}) %all-to-all-start.5) | async-done | bytes 917536 | tf_op jit(solution)/shard_map/all_to_all | solution.py:662
  (141 shorter events, 27.2 us)
Async XLA Ops:
  17.1 9.6 %copy-start.15 = (bf16[2,1024]{1,0:T(2,128)(2,1)S(1)}, bf16[2,1024]{1,0:T(2,128)(2,1)}, u32[]{:S(2)}) copy-start(bf16[2,1024]{1,0:T(2,128)(2,1)} %t_ref.1) | copy-start | bytes 12292
  17.1 33.0 %all-to-all-start = ((bf16[16,400,128]{2,1,0:T(8,128)(2,1)}), bf16[16,400,128]{2,1,0:T(8,128)(2,1)S(1)}, u32[]{:S(2)}, u32[]{:S(2)}) async-start(bf16[16,400,128]{2,1,0:T(8,128)(2,1)} %get-tuple-element.38), calls=%async_computation | async-start | bytes 3276800 | tf_op jit(solution)/shard_map/all_to_all | solution.py:662
  26.6 23.6 %copy-start.17 = (bf16[2048]{0:T(1024)(128)(2,1)S(1)}, bf16[2048]{0:T(1024)(128)(2,1)}, u32[]{:S(2)}) copy-start(bf16[2048]{0:T(1024)(128)(2,1)} %param.24) | copy-start | bytes 12292
  26.6 23.6 %copy-start.19 = (bf16[1024]{0:T(1024)(128)(2,1)S(1)}, bf16[1024]{0:T(1024)(128)(2,1)}, u32[]{:S(2)}) copy-start(bf16[1024]{0:T(1024)(128)(2,1)} %param.22) | copy-start | bytes 6148
  26.6 23.6 %copy-start.20 = (bf16[1024]{0:T(1024)(128)(2,1)S(1)}, bf16[1024]{0:T(1024)(128)(2,1)}, u32[]{:S(2)}) copy-start(bf16[1024]{0:T(1024)(128)(2,1)} %param.26) | copy-start | bytes 6148
  26.6 23.6 %copy-start.16 = (bf16[6144]{0:T(1024)(128)(2,1)S(1)}, bf16[6144]{0:T(1024)(128)(2,1)}, u32[]{:S(2)}) copy-start(bf16[6144]{0:T(1024)(128)(2,1)} %param.18) | copy-start | bytes 36868
  26.6 125.5 %all-gather.3.cloned.1.call-start = ((), (), s32[]{:S(2)}) async-start(), calls=%async_computation.8 | async-start | bytes 8912896 | tf_op jit(solution)/shard_map/all_gather | solution.py:714
  67.0 16.8 %all-to-all-start.1 = ((bf16[16,2,64,128]{3,2,1,0:T(8,128)(2,1)}), bf16[16,2,64,128]{3,2,1,0:T(8,128)(2,1)S(1)}, u32[]{:S(2)}, u32[]{:S(2)}) async-start(bf16[16,2,64,128]{3,2,1,0:T(8,128)(2,1)} %get-tuple-element.41.o_ref), calls=%async_computation.1 | async-start | bytes 1048576 | tf_op jit(solution)/shard_map/all_to_all | solution.py:662
  72.4 11.3 %copy-start.5 = (bf16[2,128,1024]{2,1,0:T(8,128)(2,1)S(1)}, bf16[2,128,1024]{2,1,0:T(8,128)(2,1)}, u32[]{:S(2)}) copy-start(bf16[2,128,1024]{2,1,0:T(8,128)(2,1)} %param.27) | copy-start | bytes 1572868
  72.4 11.3 %copy-start.6 = (bf16[2,128,1024]{2,1,0:T(8,128)(2,1)S(1)}, bf16[2,128,1024]{2,1,0:T(8,128)(2,1)}, u32[]{:S(2)}) copy-start(bf16[2,128,1024]{2,1,0:T(8,128)(2,1)} %param.14) | copy-start | bytes 1572868
  99.8 7.0 %collective-permute-start = (bf16[256,4096]{1,0:T(8,128)(2,1)}, bf16[256,4096]{1,0:T(8,128)(2,1)}, u32[]{:S(2)}, u32[]{:S(2)}) collective-permute-start(bf16[256,4096]{1,0:T(8,128)(2,1)} %get-tuple-element.43.oa.ha.aa), channel_id=1, source_target_pairs={{0,1},{1,0},{2,3},{3,2},{4,5},{5,4},{6,7},{7,6},{8,9},{9,8},{10,11... | collective-permute-start | bytes 6291464 | tf_op jit(solution)/shard_map/ppermute | solution.py:675
  101.0 5.3 %collective-permute-start.1 = (bf16[256,2048]{1,0:T(8,128)(2,1)S(1)}, bf16[256,2048]{1,0:T(8,128)(2,1)S(1)}, u32[]{:S(2)}, u32[]{:S(2)}) collective-permute-start(bf16[256,2048]{1,0:T(8,128)(2,1)S(1)} %get-tuple-element.45), channel_id=1, source_target_pairs={{0,1},{1,0},{2,3},{3,2},{4,5},{5,4},{6,7},{7,6},{8,9},{9,8},{10,11... | collective-permute-start | bytes 3145736 | tf_op jit(solution)/shard_map/ppermute | solution.py:675
  101.0 21.3 %all-to-all-start.2 = ((bf16[16,144,128]{2,1,0:T(8,128)(2,1)}), bf16[16,144,128]{2,1,0:T(8,128)(2,1)S(1)}, u32[]{:S(2)}, u32[]{:S(2)}) async-start(bf16[16,144,128]{2,1,0:T(8,128)(2,1)} %get-tuple-element.46), calls=%async_computation.2 | async-start | bytes 1179648 | tf_op jit(solution)/shard_map/all_to_all | solution.py:662
  104.9 70.1 %reduce-scatter.2.cloned.1.call-start = ((), (), s32[]{:S(2)}) async-start(), calls=%async_computation.7 | async-start | bytes 6553600 | tf_op jit(solution)/shard_map/reduce_scatter | solution.py:727
  122.3 1.8 copy-start.9
  122.3 1.8 copy-start.10
  122.3 1.8 copy-start.11
  160.5 28.8 %copy-start.14 = (bf16[1024,256]{1,0:T(8,128)(2,1)S(1)}, bf16[1024,256]{1,0:T(8,128)(2,1)}, u32[]{:S(2)}) copy-start(bf16[1024,256]{1,0:T(8,128)(2,1)} %get-tuple-element.57) | copy-start | bytes 1572868
  160.5 28.6 %all-to-all-start.3 = ((bf16[16,416,128]{2,1,0:T(8,128)(2,1)}), bf16[16,416,128]{2,1,0:T(8,128)(2,1)S(1)}, u32[]{:S(2)}, u32[]{:S(2)}) async-start(bf16[16,416,128]{2,1,0:T(8,128)(2,1)} %get-tuple-element.55), calls=%async_computation.3 | async-start | bytes 3407872 | tf_op jit(solution)/shard_map/all_to_all | solution.py:662
  176.1 22.4 %collective-permute-start.2 = (bf16[16,16,1280]{2,1,0:T(8,128)(2,1)S(1)}, bf16[16,16,1280]{2,1,0:T(8,128)(2,1)S(1)}, u32[]{:S(2)}, u32[]{:S(2)}) collective-permute-start(bf16[16,16,1280]{2,1,0:T(8,128)(2,1)S(1)} %dynamic-slice_bitcast_fusion), channel_id=1, source_target_pairs={{0,64},{16,80},{32,96},{48,112},{64,0},{80,16},{96,32},{112,48},{1... | collective-permute-start | bytes 1966088 | tf_op jit(solution)/shard_map/ppermute | solution.py:737
  189.1 18.1 %copy-start.12 = (bf16[16,416,128]{2,1,0:T(8,128)(2,1)}, bf16[16,416,128]{2,1,0:T(8,128)(2,1)S(1)}, u32[]{:S(2)}) copy-start(bf16[16,416,128]{2,1,0:T(8,128)(2,1)S(1)} %all-to-all-done.3.g_ref) | copy-start | bytes 5111812
  199.4 16.2 %all-to-all-start.4 = ((bf16[8,144,256]{2,1,0:T(8,128)(2,1)}), bf16[8,144,256]{2,1,0:T(8,128)(2,1)S(1)}, u32[]{:S(2)}, u32[]{:S(2)}) async-start(bf16[8,144,256]{2,1,0:T(8,128)(2,1)} %pad_maximum_fusion), calls=%async_computation.5 | async-start | bytes 1179648 | tf_op jit(solution)/shard_map/all_to_all | solution.py:662
  217.8 24.9 %all-to-all-start.5 = ((bf16[16,8,3584]{2,1,0:T(8,128)(2,1)}), bf16[16,8,3584]{2,1,0:T(8,128)(2,1)S(1)}, u32[]{:S(2)}, u32[]{:S(2)}) async-start(bf16[16,8,3584]{2,1,0:T(8,128)(2,1)} %concatenate.34), calls=%async_computation.6 | async-start | bytes 1835008 | tf_op jit(solution)/shard_map/all_to_all | solution.py:662
  243.0 6.6 %copy-start.18 = (f32[8,2048]{1,0:T(8,128)}, f32[8,2048]{1,0:T(8,128)S(1)}, u32[]{:S(2)}) copy-start(f32[8,2048]{1,0:T(8,128)S(1)} %constant_dynamic-update-slice_fusion.2) | copy-start | bytes 196612
  (9 other events, 10.3 us)
Sparse Core Ops, SparseCore 0:
  50.3 79.9 all-gather.2
Sparse Core Ops, SparseCore 1:
  122.4 52.5 reduce-scatter.1
